TPU v7x, 256 devices: a whole 4x4x8 slice. The times are simulated.
256 devices in a mesh: cfd: 32 (over y, z), struct: 8 (over x, core).
Axes of the slice: x: 4, y: 4, z: 8, core: 2. Of those that a mesh axis runs over, the one named last changes fastest.
Arguments:
- node_loads: bfloat16 [524288, 192], P(('cfd', 'struct')), may hold values from -6 to 6
- dest_owner: int32 [524288, 1], P(('cfd', 'struct')), may hold values from 0 to 31; in each aligned block of 2048 rows (0 to 2047, 2048 to 4095, ...) at most 256 rows name the same one
- dest_elem: int32 [524288], P(('cfd', 'struct')), may hold values from 0 to 2047
- node_weight: float32 [524288], P(('cfd', 'struct')), may hold values from 0.5 to 1.5
- mode_shapes: bfloat16 [3, 524288, 512], P(None, ('cfd', 'struct')), may hold values from -0.25 to 0.25
- stiffness: float32 [512], replicated, may hold values from 0.5 to 4
Outputs:
- node_disp: bfloat16 [524288, 192], P(('cfd', 'struct'))
- modal_amp: float32 [512, 64], replicated
Inputs may be any that keep to these rules, and one draw needn't show every extreme that they name: `dest_owner`: within the rows of one device, no owner is named by more than 256 rows, and some device names one owner exactly 256 times.
All inputs are finite; a program needn't handle non-finite values.
Results may differ from a plain program's by a relative error of at most 0.0063.
Values may be sent and summed in bfloat16 or wider, within the bound.
A program may use at most 192 MiB of HBM per device.

v0:
```python
import math

import jax
import jax.numpy as jnp
from jax import lax
from jax.sharding import PartitionSpec as P


def per_device(node_loads, dest_owner, dest_elem, node_weight, mode_shapes, stiffness):
    rows, width = node_loads.shape
    rhs_count = width // 3
    owners = lax.axis_size("cfd")
    devices = owners * lax.axis_size("struct")
    capacity = max(2, 4 * rows // owners)
    elems = mode_shapes.shape[1]
    owner = dest_owner[:, 0]
    owner_hits = (owner[:, None] == jnp.arange(owners, dtype=jnp.int32)[None, :]).astype(jnp.int32)
    earlier = jnp.cumsum(owner_hits, axis=0) - owner_hits
    rank = jnp.sum(earlier * owner_hits, axis=1)
    send_loads = jnp.zeros((owners, capacity, width), jnp.bfloat16).at[owner, rank].set(node_loads)
    send_elem = jnp.full((owners, capacity), elems, jnp.int32).at[owner, rank].set(dest_elem)
    got_loads, got_elem = (
        lax.all_to_all(send_loads, "cfd", split_axis=0, concat_axis=0, tiled=True),
        lax.all_to_all(send_elem, "cfd", split_axis=0, concat_axis=0, tiled=True),
    )
    slots = owners * capacity
    slot_loads = got_loads.reshape(slots, width)
    slot_elem = got_elem.reshape(slots)
    block = math.gcd(512, slots)
    columns = jnp.arange(elems, dtype=jnp.int32)

    def add_block(total, index):
        start = index * block
        loads = lax.dynamic_slice_in_dim(slot_loads, start, block, 0)
        target = lax.dynamic_slice_in_dim(slot_elem, start, block, 0)
        select = (columns[:, None] == target[None, :]).astype(jnp.bfloat16)
        return (total + jnp.dot(select, loads, preferred_element_type=jnp.float32), None)

    elem_sum, _ = lax.scan(
        add_block,
        jnp.zeros((elems, width), jnp.float32),
        jnp.arange(slots // block, dtype=jnp.int32),
    )
    elem_load = elem_sum.astype(jnp.bfloat16).reshape(elems, 3, rhs_count)
    partial_force = jnp.einsum(
        "kem,ekr->mr", mode_shapes, elem_load, preferred_element_type=jnp.float32
    )
    scale = jnp.sqrt(jnp.float32(3.0 * rows * devices))
    modal_force = lax.psum(partial_force, ("cfd", "struct"))
    modal_amp = modal_force / (stiffness[:, None] * scale)
    amp_low = modal_amp.astype(jnp.bfloat16)
    elem_disp = jnp.einsum("kem,mr->ekr", mode_shapes, amp_low, preferred_element_type=jnp.float32)
    elem_disp = elem_disp.reshape(elems, width).astype(jnp.bfloat16)
    slot_disp = jnp.take(elem_disp, slot_elem, axis=0, mode="fill", fill_value=0).reshape(
        owners, capacity, width
    )
    returned = lax.all_to_all(slot_disp, "cfd", split_axis=0, concat_axis=0, tiled=True)
    node_value = returned[owner, rank]
    node_disp = (node_weight[:, None] * node_value.astype(jnp.float32)).astype(jnp.bfloat16)
    return (node_disp, modal_amp)


def solution(mesh):
    placed = (
        P(("cfd", "struct"), None),
        P(("cfd", "struct"), None),
        P(("cfd", "struct")),
        P(("cfd", "struct")),
        P(None, ("cfd", "struct"), None),
        P(),
    )
    return jax.shard_map(
        per_device,
        mesh=mesh,
        in_specs=placed,
        out_specs=(P(("cfd", "struct"), None), P()),
        check_vma=False,
    )
```

profile of v0, /device:TPU:32, one launch (start us, length us, event | category | flops | bytes accessed | tf_op | source)
XLA Modules:
  0.0 614.1 jit_solution(16000298673451854955)
XLA Ops:
  7.9 9.1 %reduce-window.6 = s32[32,16,128]{2,1,0:T(8,128)S(1)} reduce-window(s32[32,16,128]{2,1,0:T(8,128)S(1)} %fusion.12, s32[]{:T(128)} %constant.22.clone.1), window={size=1x1x128 pad=0_0x0_0x127_0}, to_apply=%region_0.0 | reduce-window | flops 8323072 | bytes 524292 | tf_op jit(solution)/shard_map/reduce-window
  20.8 8.8 %scatter_custom_fusion = s32[8192]{0:T(1024)} fusion(s32[2048]{0:T(1024)S(1)} %broadcast_select_fusion.1, s32[2048]{0:T(1024)} %param.10, s32[]{:T(128)} %constant.21.clone.1), kind=kCustom, calls=%fused_computation.36 | custom fusion | bytes 33280
  29.6 11.4 %all-to-all-start = ((s32[32,1,256]{2,1,0:T(1,128)}), s32[32,1,256]{2,1,0:T(1,128)S(1)}, u32[]{:S(2)}, u32[]{:S(2)}) async-start(s32[32,1,256]{2,1,0:T(1,128)} %bitcast.6), calls=%async_computation | async-start | bytes 65536 | tf_op jit(solution)/shard_map/all_to_all | solution.py:24
  42.4 12.0 %scatter_custom_fusion.1 = bf16[8192,192]{1,0:T(8,128)(2,1)} fusion(s32[2048]{0:T(1024)S(1)} %broadcast_select_fusion.1, bf16[2048,192]{1,0:T(8,128)(2,1)S(1)} %copy.25, bf16[]{:T(256)} %constant.41.clone.1), kind=kCustom, calls=%fused_computation.13 | custom fusion | bytes 3145730
  54.3 6.2 %copy.26 = bf16[32,256,192]{1,2,0:T(8,128)(2,1)} copy(bf16[32,256,192]{2,1,0:T(8,128)(2,1)} %bitcast.53) | data formatting | bytes 6291456 | tf_op jit(solution)/shard_map/scatter | solution.py:20
  60.6 10.0 %all-to-all-start.1 = ((bf16[32,256,192]{1,2,0:T(8,128)(2,1)}), bf16[32,256,192]{1,2,0:T(8,128)(2,1)}, u32[]{:S(2)}, u32[]{:S(2)}) async-start(bf16[32,256,192]{1,2,0:T(8,128)(2,1)} %copy.26), calls=%async_computation.1 | async-start | bytes 6291456 | tf_op jit(solution)/shard_map/all_to_all | solution.py:23
  70.9 69.3 %all-to-all-done.1 = bf16[32,256,192]{1,2,0:T(8,128)(2,1)} async-done(((bf16[32,256,192]{1,2,0:T(8,128)(2,1)}), bf16[32,256,192]{1,2,0:T(8,128)(2,1)}, u32[]{:S(2)}, u32[]{:S(2)}) %all-to-all-start.1) | async-done | bytes 3145760 | tf_op jit(solution)/shard_map/all_to_all | solution.py:23
  140.2 6.1 copy.34
  146.3 57.2 %while.11 = (s32[]{:T(128)}, f32[2048,192]{0,1:T(8,128)S(1)}, s32[16]{0:T(128)S(1)}, s32[8192]{0:T(1024)S(1)}, bf16[8192,192]{1,0:T(8,128)(2,1)}, /*index=5*/s32[]{:T(128)}, s32[1]{0:T(128)}, s32[]{:T(128)}, s32[]{:T(128)}) while((s32[]{:T(128)}, f32[2048,192]{0,1:T(8,128)S(1)}, s32[16]{0:T(128)S(1)}, s32[8192]{0:T(1024)S(1)}, ...), condition=%wide.region_6.7_spmd.clone, body=%wide.region_5.6_spmd.clone.sunk | while | flops 404488192 | bytes 3414185 | solution.py:39
  151.2 2.2 fusion.23
  154.8 2.2 fusion.23
  158.4 2.2 fusion.23
  162.0 2.2 fusion.23
  165.5 2.2 fusion.23
  169.1 2.2 fusion.23
  172.7 2.2 fusion.23
  176.3 2.2 fusion.23
  179.9 2.2 fusion.23
  183.4 2.2 fusion.23
  187.0 2.2 fusion.23
  190.6 2.2 fusion.23
  194.2 2.2 fusion.23
  197.8 2.2 fusion.23
  201.3 2.2 fusion.23
  203.7 4.6 convolution_bitcast_fusion
  208.4 241.3 %all-reduce.2.cloned.1.call-done = f32[512,64]{0,1:T(8,128)} async-done(((f32[512,64]{0,1:T(8,128)}), f32[512,64]{0,1:T(8,128)}) %all-reduce.2.cloned.1.call-update) | async-done | bytes 131088 | tf_op jit(solution)/shard_map/psum | solution.py:49
  450.7 4.8 convolution_convert_fusion
  456.0 32.9 %gather_fusion = bf16[8192,192]{1,0:T(8,128)(2,1)} fusion(bf16[2048,192]{1,0:T(8,128)(2,1)S(1)} %copy.29, s32[8192]{0:T(1024)S(1)} %broadcast_clamp_fusion), kind=kCustom, calls=%fused_computation | custom fusion | bytes 6324224 | tf_op jit(solution)/shard_map/jit(_take)/gather | solution.py:54
  488.9 5.5 copy.30
  494.6 81.0 %all_to_all.19 = bf16[32,256,192]{1,2,0:T(8,128)(2,1)S(1)} all-to-all(bf16[32,256,192]{1,2,0:T(8,128)(2,1)S(1)} %broadcast_select_fusion), channel_id=1, replica_groups=mesh['cfd'=32,'struct'=8] {'cfd'}, dimensions={0} | all-to-all | bytes 6291456 | tf_op jit(solution)/shard_map/all_to_all | solution.py:57
  575.6 4.6 copy.31
  580.2 25.4 %gather_fusion.1 = bf16[2048,192]{1,0:T(8,128)(2,1)S(1)} fusion(bf16[32,256,192]{2,1,0:T(8,128)(2,1)} %copy.31, s32[2048]{0:T(1024)S(1)} %bitcast.52), kind=kCustom, calls=%fused_computation.1 | custom fusion | bytes 1589248 | tf_op jit(solution)/shard_map/gather | solution.py:58
  (65 shorter events, 22.5 us)
Async XLA Ops:
  29.6 31.0 %all-to-all-start = ((s32[32,1,256]{2,1,0:T(1,128)}), s32[32,1,256]{2,1,0:T(1,128)S(1)}, u32[]{:S(2)}, u32[]{:S(2)}) async-start(s32[32,1,256]{2,1,0:T(1,128)} %bitcast.6), calls=%async_computation | async-start | bytes 65536 | tf_op jit(solution)/shard_map/all_to_all | solution.py:24
  60.6 10.2 %copy-start.2 = (f32[512]{0:T(512)S(1)}, f32[512]{0:T(512)}, u32[]{:S(2)}) copy-start(f32[512]{0:T(512)} %param.13) | copy-start | bytes 6148
  60.6 79.6 %all-to-all-start.1 = ((bf16[32,256,192]{1,2,0:T(8,128)(2,1)}), bf16[32,256,192]{1,2,0:T(8,128)(2,1)}, u32[]{:S(2)}, u32[]{:S(2)}) async-start(bf16[32,256,192]{1,2,0:T(8,128)(2,1)} %copy.26), calls=%async_computation.1 | async-start | bytes 6291456 | tf_op jit(solution)/shard_map/all_to_all | solution.py:23
  70.6 379.2 %all-reduce.2.cloned.1.call-start = ((), (), s32[]{:S(2)}) async-start(), calls=%async_computation.3 | async-start | bytes 262144 | tf_op jit(solution)/shard_map/psum | solution.py:49
  450.6 5.4 copy-start
  580.2 25.5 %copy-start.1 = (f32[2048]{0:T(1024)S(1)}, f32[2048]{0:T(1024)}, u32[]{:S(2)}) copy-start(f32[2048]{0:T(1024)} %param.11) | copy-start | bytes 24580
Sparse Core Ops, SparseCore 0:
  208.5 241.1 all-reduce.1
where the time goes:
time: 616 us; the launch traced here: 614 us
  waiting for transfers between devices  311 us (50%)
  local copies, waits for them, and re-layouts  116 us (19%)
  blocking collectives  81 us (13%)
  matrix products  45.2 us (7%)
  starting transfers between devices  21.5 us (3%)
  other arithmetic  14.9 us (2%)
  between operations  14.2 us (2%)
  loops' own time  10.9 us (2%)
    psum x1, waiting for transfers between devices, per_device(): modal_force = lax.psum(partial_force, ('cfd', 'struct'))  241 us
    all_to_all x1, blocking collectives, per_device(): lax.all_to_all(slot_disp, 'cfd', split_axis=0, concat_axis=0, tiled=True)  81 us
    all_to_all x1, waiting for transfers between devices, per_device(): lax.all_to_all(send_loads, 'cfd', split_axis=0, concat_axis=0, tiled=True)  69.3 us
    gather x2, local copies, waits for them, and re-layouts, per_device(): jnp.take(elem_disp, slot_elem, axis=0, mode='fill', fill_value=0)  38.4 us
    dot_general x16, matrix products, add_block(): jnp.dot(select, loads, preferred_element_type=jnp.float32)  35.8 us
    unnamed x11, local copies, waits for them, and re-layouts  29.5 us
    gather x1, local copies, waits for them, and re-layouts, per_device(): node_value = returned[owner, rank]  25.4 us
  transfers between devices with their start and end apart: 3, of which 2 were waited for; matrix products, arithmetic and copies ran while one was open for 3% of the time, Pallas kernels for 0%

commit v1 on v0

--- a/solution.py
+++ b/solution.py
@@ -1,12 +1,20 @@
+import functools
 import math
 
 import jax
 import jax.numpy as jnp
+import numpy as np
 from jax import lax
+from jax.experimental import pallas as pl
+from jax.experimental.pallas import tpu as pltpu
 from jax.sharding import PartitionSpec as P
 
-
-def per_device(node_loads, dest_owner, dest_elem, node_weight, mode_shapes, stiffness):
+MESH = pl.DeviceIdType.MESH
+BF16, F32, I32 = jnp.bfloat16, jnp.float32, jnp.int32
+CLASS_CAP = 128
+
+
+def general(node_loads, dest_owner, dest_elem, node_weight, mode_shapes, stiffness):
     rows, width = node_loads.shape
     rhs_count = width // 3
     owners = lax.axis_size("cfd")
@@ -60,6 +68,481 @@
     return (node_disp, modal_amp)
 
 
+def mm(a, b):
+    return jnp.dot(a, b, preferred_element_type=F32)
+
+
+def iota(shape, dim):
+    return lax.broadcasted_iota(I32, shape, dim)
+
+
+def column(row):
+    return jnp.transpose(jnp.broadcast_to(row, (128, 128)))
+
+
+def split_halves(tail):
+    low = iota(tail.shape, 1) < 64
+    zero = jnp.zeros_like(tail)
+    return jnp.concatenate([jnp.where(low, tail, zero), jnp.where(low, zero, tail)], axis=0)
+
+
+def fused_kernel(
+    n, ny, ns, nodes_scale,
+    owner_ref, elem_ref, weight_ref, loads_ref, stiff_ref, mode_ref,
+    out_ref, amp_ref,
+    rows_ref, slot_ref, poison_ref, send1, keys_out, recv1, keys_in, acc, send2, recv2,
+    mode_v, force, piece_out, piece_in, ring_out, ring_in, total_in,
+    send3, recv3, disp, send4, recv4, slot_col, weight_col,
+    s1, r1, k1, q1, s2, r2, sa, ra, sb, rb, sc, rc, s3, r3, s4, r4, mode_sem,
+):
+    nz = n // ny
+    me = lax.axis_index("cfd")
+    st = lax.axis_index("struct")
+    my_y, my_z = me // nz, lax.rem(me, nz)
+    my_q = my_y * ns + st
+    group = ny * ns
+    count = rows_ref.shape[0]
+
+    def cfd_peer(t):
+        return lax.rem(me + t, n)
+
+    def plane_peer(t):
+        q = lax.rem(my_q + t, group)
+        return q, ((q // ns) * nz + my_z, lax.rem(q, ns))
+
+    def z_peer(t):
+        z = lax.rem(my_z + t, nz)
+        return z, (my_y * nz + z, st)
+
+    barrier = pltpu.get_barrier_semaphore()
+
+    def greet_cfd(t, _):
+        pl.semaphore_signal(barrier, inc=1, device_id=(cfd_peer(t), st), device_id_type=MESH)
+        return 0
+
+    def greet_plane(t, _):
+        other = lax.rem(st + 1 + lax.rem(t, ns - 1), ns)
+        pl.semaphore_signal(
+            barrier, inc=1, device_id=(t // (ns - 1) * nz + my_z, other), device_id_type=MESH)
+        return 0
+
+    lax.fori_loop(1, n, greet_cfd, 0)
+    lax.fori_loop(0, ny * (ns - 1), greet_plane, 0)
+    mode_copy = pltpu.make_async_copy(mode_ref, mode_v, mode_sem)
+    mode_copy.start()
+
+    owner = owner_ref[...]
+    elem = elem_ref[...]
+    cls = lax.rem(elem // 64 + owner, n)
+    upper = (iota((256, 256), 0) < iota((256, 256), 1)).astype(BF16)
+    base = jnp.zeros((n, 1), F32)
+    for q in range(count // 256):
+        part = cls[:, 256 * q : 256 * q + 256]
+        hit = iota((n, 256), 0) == jnp.broadcast_to(part, (n, 256))
+        hit_f = hit.astype(F32)
+        before = mm(hit_f.astype(BF16), upper) + base
+        rank = jnp.sum(jnp.where(hit, before, 0.0), axis=0, keepdims=True).astype(I32)
+        slot_ref[:, 256 * q : 256 * q + 256] = jnp.where(rank < CLASS_CAP, part * CLASS_CAP + rank, -1)
+        base = base + jnp.sum(hit_f, axis=1, keepdims=True)
+    most = jnp.max(base, axis=0, keepdims=True)
+    poison_ref[...] = jnp.broadcast_to(jnp.where(most > CLASS_CAP, jnp.nan, 0.0), (8, 128))
+
+    for q in range(count // 128):
+        cols = slice(128 * q, 128 * q + 128)
+        sub = iota((128, 128), 0)
+        own = jnp.broadcast_to((owner[:, cols] + 1).astype(F32), (128, 128))
+        low = jnp.broadcast_to(lax.rem(elem[:, cols], 64).astype(F32), (128, 128))
+        meta = jnp.transpose(jnp.where(sub == 64, own, jnp.where(sub == 65, low, 0.0)))
+        rows_ref[cols, 0:128] = loads_ref[cols, 0:128]
+        tail = jnp.concatenate([loads_ref[cols, 128:192], jnp.zeros((128, 64), BF16)], axis=1)
+        rows_ref[cols, 128:256] = tail + meta.astype(BF16)
+
+    pl.semaphore_wait(barrier, n - 1 + group - ny)
+
+    def hop1(peer, src):
+        return pltpu.make_async_remote_copy(
+            src_ref=send1.at[peer], dst_ref=recv1.at[src], send_sem=s1.at[peer], recv_sem=r1.at[src],
+            device_id=(peer, st), device_id_type=MESH)
+
+    def hop1_keys(peer, src):
+        return pltpu.make_async_remote_copy(
+            src_ref=keys_out.at[peer], dst_ref=keys_in.at[src], send_sem=k1.at[peer], recv_sem=q1.at[src],
+            device_id=(peer, st), device_id_type=MESH)
+
+    def build(c):
+        slots = jnp.broadcast_to(slot_ref[...] - c * CLASS_CAP, (128, count))
+        pick = (slots == iota((128, count), 0)).astype(BF16)
+        y = mm(pick, rows_ref[...])
+        tail = y[:, 128:256]
+        send1[c, 0:128, :] = y[:, 0:128].astype(BF16)
+        low = iota((64, 128), 1) < 64
+        send1[c, 128:192, :] = jnp.where(low, tail[0:64], pltpu.roll(tail[64:128], 64, 1)).astype(BF16)
+        turned = jnp.transpose(tail)
+        keys_out[c] = (turned[64:65] * 64.0 + turned[65:66] - 64.0).astype(I32)
+
+    def start1(t, _):
+        c = cfd_peer(t)
+        build(c)
+        hop1(c, me).start()
+        hop1_keys(c, me).start()
+        return 0
+
+    lax.fori_loop(1, n, start1, 0)
+    build(me)
+    recv1[me] = send1[me]
+    keys_in[me] = keys_out[me]
+
+    acc[...] = jnp.zeros_like(acc)
+
+    def combine(g, _):
+        keys, parts = [], []
+        for u in range(4):
+            t = g * 4 + u
+            src = lax.rem(me + n - t, n)
+
+            @pl.when(t > 0)
+            def _():
+                hop1(src, src).wait_recv()
+                hop1_keys(src, src).wait_recv()
+
+            keys.append(keys_in[src])
+            parts.append(jnp.concatenate([recv1[src, 0:128, :], split_halves(recv1[src, 128:192, :])], axis=1))
+        keys = jnp.concatenate(keys, axis=1)
+        parts = jnp.concatenate(parts, axis=0)
+
+        def block(b, _):
+            at = pl.ds(pl.multiple_of(b * 256, 256), 256)
+            hit = jnp.broadcast_to(keys - b * 256, (256, 512)) == iota((256, 512), 0)
+            acc[at, :] += mm(hit.astype(BF16), parts)
+            return 0
+
+        lax.fori_loop(0, acc.shape[0] // 256, block, 0)
+        return 0
+
+    lax.fori_loop(0, n // 4, combine, 0)
+
+    def hop2(peer, src):
+        return pltpu.make_async_remote_copy(
+            src_ref=send2.at[peer], dst_ref=recv2.at[src], send_sem=s2.at[peer], recv_sem=r2.at[src],
+            device_id=(peer, st), device_id_type=MESH)
+
+    def pack2(d):
+        at = pl.ds(pl.multiple_of(d * 64, 64), 64)
+        send2[d, 0:64, :] = acc[at, 0:128].astype(BF16)
+        tail = acc[at, 128:256]
+        tail = tail + pltpu.roll(tail, 64, 1)
+        low = iota((32, 128), 1) < 64
+        send2[d, 64:96, :] = jnp.where(low, tail[0:32], tail[32:64]).astype(BF16)
+
+    def start2(t, _):
+        d = cfd_peer(t)
+        pack2(d)
+        hop2(d, me).start()
+        return 0
+
+    lax.fori_loop(1, n, start2, 0)
+    pack2(me)
+    recv2[me] = send2[me]
+
+    for q in range(count // 128):
+        cols = slice(128 * q, 128 * q + 128)
+        slot_col[cols, :] = column(slot_ref[:, cols].astype(F32)).astype(I32)
+        weight_col[cols, :] = column(weight_ref[:, cols])
+
+    mode_copy.wait()
+    force[...] = jnp.zeros_like(force)
+
+    def project(g, _):
+        parts = []
+        for u in range(4):
+            b = g * 4 + u
+            blk = n - 1 - b
+            src = lax.rem(me + blk, n)
+
+            @pl.when(blk > 0)
+            def _():
+                hop2(src, src).wait_recv()
+
+            tail = recv2[src, 64:96, :]
+            low = iota((32, 128), 1) < 64
+            zero = jnp.zeros_like(tail)
+            tail = jnp.concatenate([jnp.where(low, tail, zero), jnp.where(low, zero, tail)], axis=0)
+            parts.append(jnp.concatenate([recv2[src, 0:64, :], tail], axis=1))
+        load = jnp.concatenate(parts[::-1], axis=0)
+        load = jnp.transpose(load.astype(F32)).astype(BF16)
+        at = pl.ds(pl.multiple_of((n // 4 - 1 - g) * 256, 256), 256)
+        f0 = mm(load[0:64], mode_v[0, at, :])
+        f1 = mm(load[64:128], mode_v[1, at, :])
+        f2 = mm(load[128:256], mode_v[2, at, :])
+        force[...] += f0 + f1 + f2[0:64] + f2[64:128]
+        return 0
+
+    lax.fori_loop(0, n // 4, project, 0)
+
+    rt = force.shape[0] // 8
+    ct = force.shape[1] // 128
+    for p in range(rt * ct):
+        i, j = p // ct, p % ct
+        piece_out[p] = force[8 * i : 8 * i + 8, 128 * j : 128 * j + 128] + poison_ref[...]
+
+    def hop_a(q, dev, src):
+        return pltpu.make_async_remote_copy(
+            src_ref=piece_out.at[q], dst_ref=piece_in.at[src], send_sem=sa.at[q], recv_sem=ra.at[src],
+            device_id=dev, device_id_type=MESH)
+
+    def start_a(t, _):
+        q, dev = plane_peer(t)
+        hop_a(q, dev, my_q).start()
+        return 0
+
+    lax.fori_loop(1, group, start_a, 0)
+    piece_in[my_q] = piece_out[my_q]
+
+    def wait_a(t, _):
+        q, dev = plane_peer(group - t)
+        hop_a(q, dev, q).wait_recv()
+        return 0
+
+    lax.fori_loop(1, group, wait_a, 0)
+    ring_out[...] = jnp.sum(piece_in[...], axis=0)
+
+    def hop_b(z, dev, src):
+        return pltpu.make_async_remote_copy(
+            src_ref=ring_out, dst_ref=ring_in.at[src], send_sem=sb.at[z], recv_sem=rb.at[src],
+            device_id=dev, device_id_type=MESH)
+
+    def start_b(t, _):
+        z, dev = z_peer(t)
+        hop_b(z, dev, my_z).start()
+        return 0
+
+    lax.fori_loop(1, nz, start_b, 0)
+    ring_in[my_z] = ring_out[...]
+
+    def wait_b(t, _):
+        z, dev = z_peer(nz - t)
+        hop_b(z, dev, z).wait_recv()
+        return 0
+
+    lax.fori_loop(1, nz, wait_b, 0)
+    total_in[my_q] = jnp.sum(ring_in[...], axis=0)
+
+    def hop_c(q, dev):
+        return pltpu.make_async_remote_copy(
+            src_ref=total_in.at[my_q], dst_ref=total_in.at[my_q], send_sem=sc.at[q], recv_sem=rc.at[my_q],
+            device_id=dev, device_id_type=MESH)
+
+    def got_c(q, dev):
+        return pltpu.make_async_remote_copy(
+            src_ref=total_in.at[q], dst_ref=total_in.at[q], send_sem=sc.at[q], recv_sem=rc.at[q],
+            device_id=dev, device_id_type=MESH)
+
+    def start_c(t, _):
+        q, dev = plane_peer(t)
+        hop_c(q, dev).start()
+        return 0
+
+    lax.fori_loop(1, group, start_c, 0)
+
+    def wait_c(t, _):
+        q, dev = plane_peer(group - t)
+        got_c(q, dev).wait_recv()
+        return 0
+
+    lax.fori_loop(1, group, wait_c, 0)
+    whole = jnp.concatenate(
+        [jnp.concatenate([total_in[i * ct + j] for j in range(ct)], axis=1) for i in range(rt)], axis=0)
+    amp_t = whole / (stiff_ref[...] * nodes_scale)
+    amp = jnp.transpose(jnp.concatenate([amp_t, amp_t], axis=0))
+    amp_ref[...] = amp[:, 0:64]
+    both = amp.astype(BF16)
+    low = iota(amp.shape, 1) < 64
+    left = jnp.where(low, amp, 0.0).astype(BF16)
+    right = jnp.where(low, 0.0, amp).astype(BF16)
+
+    def hop3(peer, src):
+        return pltpu.make_async_remote_copy(
+            src_ref=send3.at[peer], dst_ref=recv3.at[src], send_sem=s3.at[peer], recv_sem=r3.at[src],
+            device_id=(peer, st), device_id_type=MESH)
+
+    def expand(g, _):
+        at = pl.ds(pl.multiple_of(g * 256, 256), 256)
+        d01 = (mm(mode_v[0, at, :], left) + mm(mode_v[1, at, :], right)).astype(BF16)
+        d2 = mm(mode_v[2, at, :], both)
+        for u in range(4):
+            b = g * 4 + u
+            peer = cfd_peer(b)
+            send3[peer, 0:64, :] = d01[64 * u : 64 * u + 64]
+            keep = iota((32, 128), 1) < 64
+            send3[peer, 64:96, :] = jnp.where(
+                keep, d2[64 * u : 64 * u + 32], d2[64 * u + 32 : 64 * u + 64]).astype(BF16)
+
+            @pl.when(b > 0)
+            def _():
+                hop3(peer, me).start()
+
+        return 0
+
+    lax.fori_loop(0, n // 4, expand, 0)
+    recv3[me] = send3[me]
+
+    def unpack3(t, _):
+        src = lax.rem(me + n - t, n)
+
+        @pl.when(t > 0)
+        def _():
+            hop3(src, src).wait_recv()
+
+        at = pl.multiple_of(src * 64, 64)
+        disp[pl.ds(at, 64), 0:128] = recv3[src, 0:64, :]
+        tail = recv3[src, 64:96, :].astype(F32)
+        other = pltpu.roll(tail, 64, 1)
+        keep = iota((32, 128), 1) < 64
+        disp[pl.ds(at, 32), 128:256] = jnp.where(keep, tail, other).astype(BF16)
+        disp[pl.ds(at + 32, 32), 128:256] = jnp.where(keep, other, tail).astype(BF16)
+        return 0
+
+    lax.fori_loop(0, n, unpack3, 0)
+
+    def hop4(peer, src):
+        return pltpu.make_async_remote_copy(
+            src_ref=send4.at[peer], dst_ref=recv4.at[src], send_sem=s4.at[peer], recv_sem=r4.at[src],
+            device_id=(peer, st), device_id_type=MESH)
+
+    def gather(src):
+        keys = column(keys_in[src].astype(F32)).astype(I32)
+        lane = iota((128, 128), 1)
+        pick = jnp.concatenate(
+            [(keys - 128 * q == lane).astype(BF16) for q in range(disp.shape[0] // 128)], axis=1)
+        y = mm(pick, disp[...])
+        keep = iota((64, 128), 1) < 64
+        send4[src, 0:128, :] = y[:, 0:128].astype(BF16)
+        send4[src, 128:192, :] = jnp.where(keep, y[0:64, 128:256], y[64:128, 128:256]).astype(BF16)
+
+    def start4(t, _):
+        src = cfd_peer(t)
+        gather(src)
+        hop4(src, me).start()
+        return 0
+
+    lax.fori_loop(1, n, start4, 0)
+    gather(me)
+    recv4[me] = send4[me]
+
+    acc[...] = jnp.zeros_like(acc)
+
+    def place(g, _):
+        parts, firsts = [], []
+        for u in range(4):
+            t = g * 4 + u
+            src = lax.rem(me + n - t, n)
+
+            @pl.when(t > 0)
+            def _():
+                hop4(src, src).wait_recv()
+
+            firsts.append(src * CLASS_CAP)
+            parts.append(jnp.concatenate([recv4[src, 0:128, :], split_halves(recv4[src, 128:192, :])], axis=1))
+        parts = jnp.concatenate(parts, axis=0)
+
+        def block(b, _):
+            at = pl.ds(pl.multiple_of(b * 256, 256), 256)
+            slots = slot_col[at, :]
+            lane = iota((256, 128), 1)
+            pick = jnp.concatenate([(slots - first == lane).astype(BF16) for first in firsts], axis=1)
+            acc[at, :] += mm(pick, parts)
+            return 0
+
+        lax.fori_loop(0, count // 256, block, 0)
+        return 0
+
+    lax.fori_loop(0, n // 4, place, 0)
+
+    def finish(b, _):
+        at = pl.ds(pl.multiple_of(b * 256, 256), 256)
+        w = weight_col[at, :]
+        out_ref[at, 0:128] = (acc[at, 0:128] * w).astype(BF16)
+        tail = acc[at, 128:256]
+        tail = (tail + pltpu.roll(tail, 64, 1)) * w
+        out_ref[at, 128:192] = tail[:, 0:64].astype(BF16)
+        return 0
+
+    lax.fori_loop(0, count // 256, finish, 0)
+
+    def sent(t, _):
+        peer = cfd_peer(t)
+        hop1(peer, me).wait_send()
+        hop1_keys(peer, me).wait_send()
+        hop2(peer, me).wait_send()
+        hop3(peer, me).wait_send()
+        hop4(peer, me).wait_send()
+        return 0
+
+    lax.fori_loop(1, n, sent, 0)
+
+    def sent_plane(t, _):
+        q, dev = plane_peer(t)
+        hop_a(q, dev, my_q).wait_send()
+        hop_c(q, dev).wait_send()
+        return 0
+
+    lax.fori_loop(1, group, sent_plane, 0)
+
+    def sent_z(t, _):
+        z, dev = z_peer(t)
+        hop_b(z, dev, my_z).wait_send()
+        return 0
+
+    lax.fori_loop(1, nz, sent_z, 0)
+
+
+def fast(node_loads, dest_owner, dest_elem, node_weight, mode_shapes, stiffness):
+    rows, width = node_loads.shape
+    n, ns = lax.axis_size("cfd"), lax.axis_size("struct")
+    ny = 4
+    nz = n // ny
+    group = ny * ns
+    comps, elems, modes = mode_shapes.shape
+    scale = float(np.sqrt(np.float32(3.0 * rows * n * ns)))
+    vmem = pl.BlockSpec(memory_space=pltpu.VMEM)
+    dma = pltpu.SemaphoreType.DMA
+    pair = (n, 192, 128)
+    dense = (n, 96, 128)
+    return pl.pallas_call(
+        functools.partial(fused_kernel, n, ny, ns, scale),
+        out_shape=(jax.ShapeDtypeStruct((rows, width), BF16), jax.ShapeDtypeStruct((modes, 64), F32)),
+        in_specs=[vmem] * 5 + [pl.BlockSpec(memory_space=pl.ANY)],
+        out_specs=(vmem, vmem),
+        scratch_shapes=[
+            pltpu.VMEM((rows, 256), BF16), pltpu.VMEM((1, rows), I32), pltpu.VMEM((8, 128), F32),
+            pltpu.VMEM(pair, BF16), pltpu.VMEM((n, 1, 128), I32),
+            pltpu.VMEM(pair, BF16), pltpu.VMEM((n, 1, 128), I32),
+            pltpu.VMEM((rows, 256), F32), pltpu.VMEM(dense, BF16), pltpu.VMEM(dense, BF16),
+            pltpu.VMEM(mode_shapes.shape, BF16), pltpu.VMEM((64, modes), F32),
+            pltpu.VMEM((group, 8, 128), F32), pltpu.VMEM((group, 8, 128), F32),
+            pltpu.VMEM((8, 128), F32), pltpu.VMEM((nz, 8, 128), F32), pltpu.VMEM((group, 8, 128), F32),
+            pltpu.VMEM(dense, BF16), pltpu.VMEM(dense, BF16), pltpu.VMEM((elems, 256), BF16),
+            pltpu.VMEM(pair, BF16), pltpu.VMEM(pair, BF16),
+            pltpu.VMEM((rows, 128), I32), pltpu.VMEM((rows, 128), F32),
+            dma((n,)), dma((n,)), dma((n,)), dma((n,)), dma((n,)), dma((n,)),
+            dma((group,)), dma((group,)), dma((nz,)), dma((nz,)), dma((group,)), dma((group,)),
+            dma((n,)), dma((n,)), dma((n,)), dma((n,)), dma(()),
+        ],
+        compiler_params=pltpu.CompilerParams(
+            collective_id=0, has_side_effects=True, vmem_limit_bytes=56 * 1024 * 1024),
+        cost_estimate=pl.CostEstimate(flops=30_000_000_000, bytes_accessed=10_000_000, transcendentals=0),
+    )(
+        dest_owner.reshape(1, rows), dest_elem.reshape(1, rows), node_weight.reshape(1, rows),
+        node_loads, stiffness.reshape(1, modes), mode_shapes,
+    )
+
+
+def per_device(*args):
+    node_disp, modal_amp = fast(*args)
+    crowded = jnp.isnan(modal_amp[0, 0])
+    return lax.cond(crowded, lambda a, f: general(*a), lambda a, f: f, args, (node_disp, modal_amp))
+
+
 def solution(mesh):
     placed = (
         P(("cfd", "struct"), None),

time: 616 us -> 175 us (0.28)
  waiting for transfers between devices: 311 us -> 0 us
  Pallas kernels: 0 us -> 155 us
  local copies, waits for them, and re-layouts: 116 us -> 4.91 us
  blocking collectives: 81 us -> 0 us
  matrix products: 45.2 us -> 0 us
  starting transfers between devices: 21.5 us -> 0 us
  other arithmetic: 14.9 us -> 0 us
  loops' own time: 10.9 us -> 0.02 us
    psum x1 -> x0, waiting for transfers between devices: 241 us -> none  [per_device(): modal_force = lax.psum(partial_force, ('cfd', 'struct'))]
    pallas_call x0 -> x1, Pallas kernels: none -> 155 us  [fast(): pl.pallas_call(functools.partial(fused_kernel, n, ny, ns, scale), out_sha...]
    all_to_all x1 -> x0, blocking collectives: 81 us -> none  [per_device(): lax.all_to_all(slot_disp, 'cfd', split_axis=0, concat_axis=0, tiled=True)]
    all_to_all x2 -> x0, waiting for transfers between devices: 69.3 us -> none  [the longest x1 69.3 us: per_device(): lax.all_to_all(send_loads, 'cfd', split_axis=0, concat_axis=0, tiled=True)]
    gather x3 -> x0, local copies, waits for them, and re-layouts: 63.8 us -> none  [the longest x2 38.4 us: per_device(): jnp.take(elem_disp, slot_elem, axis=0, mode='fill', fill_value=0)]
    dot_general x18 -> x0, matrix products: 45.2 us -> none  [the longest x16 35.8 us: add_block(): jnp.dot(select, loads, preferred_element_type=jnp.float32)]
    unnamed x11 -> x9, local copies, waits for them, and re-layouts: 29.5 us -> 3.13 us
    all_to_all x2 -> x0, starting transfers between devices: 21.3 us -> none  [the longest x1 11.4 us: per_device(): lax.all_to_all(send_elem, 'cfd', split_axis=0, concat_axis=0, tiled=True)]
  transfers between devices with their start and end apart: 3 -> 0, of which waited for: 2 -> 0; matrix products, arithmetic and copies ran while one was open for 3% -> 0% of each run, Pallas kernels for 0% -> 0%
where the time goes in v1:
time: 175 us
  Pallas kernels  155 us (89%)
  between operations  15.3 us (9%)
  local copies, waits for them, and re-layouts  4.91 us (3%)
    pallas_call x1, Pallas kernels, fast(): pl.pallas_call(functools.partial(fused_kernel, n, ny, ns, scale), out_sha...  155 us

profile of v1, /device:TPU:32, one launch (start us, length us, event | category | flops | bytes accessed | tf_op | source)
XLA Modules:
  0.0 175.1 jit_solution(1104782674315314193)
XLA Ops:
  7.2 2.2 %copy.49.loads_ref = bf16[2048,192]{1,0:T(8,128)(2,1)} copy(bf16[2048,192]{0,1:T(8,128)(2,1)} %param.10) | data formatting | bytes 1572864 | tf_op args[0]
  9.4 0.0 copy-start
  9.4 0.0 copy-start.3
  9.4 0.0 copy-start.5
  9.4 154.9 %shard_map.81 = (bf16[2048,192]{1,0:T(8,128)(2,1)S(1)}, f32[512,64]{1,0:T(8,128)S(1)}) custom-call(s32[1,2048]{1,0:T(1,128)} %bitcast.68, s32[1,2048]{1,0:T(1,128)} %bitcast.76, f32[1,2048]{1,0:T(1,128)} %bitcast.74, bf16[2048,192]{1,0:T(8,128)(2,1)} %copy.49.loads_ref, f32[1,512]{1,0:T(1,128)} %bitcast.75, bf16[3,2048,512]{2,1,0:T(8,128)(2,1)} %mode_ref.1), custom_call_target="tpu_custom_call" | custom-call | flops 30000001024 | bytes 10000000 | tf_op jit(solution)/shard_map/pallas_call | solution.py:511
  164.3 0.5 slice.9
  166.1 0.0 copy-done
  166.1 0.0 copy-done.3
  166.1 0.0 copy-done.5
  166.1 1.3 conditional.1
  166.1 0.5 copy.55
  166.6 0.8 copy.57
  167.4 0.0 copy-start.1
  167.4 0.9 copy-done.1
Async XLA Ops:
  9.4 156.7 %copy-start = (bf16[2048,192]{0,1:T(8,128)(2,1)S(1)}, bf16[2048,192]{0,1:T(8,128)(2,1)}, u32[]{:S(2)}) copy-start(bf16[2048,192]{0,1:T(8,128)(2,1)} %param.10) | copy-start | bytes 2359300
  9.4 156.7 %copy-start.3 = (s32[2048,1]{0,1:T(1,128)S(1)}, s32[2048,1]{0,1:T(1,128)}, u32[]{:S(2)}) copy-start(s32[2048,1]{0,1:T(1,128)} %param.11) | copy-start | bytes 24580
  9.4 156.7 %copy-start.5 = (f32[512]{0:T(512)S(1)}, f32[512]{0:T(512)}, u32[]{:S(2)}) copy-start(f32[512]{0:T(512)} %param.15) | copy-start | bytes 6148
  167.4 0.9 copy-start.1

commit v2 on v1

--- a/solution.py
+++ b/solution.py
@@ -11,7 +11,8 @@
 
 MESH = pl.DeviceIdType.MESH
 BF16, F32, I32 = jnp.bfloat16, jnp.float32, jnp.int32
-CLASS_CAP = 128
+CLASS_CAP = 112
+BLOCK = CLASS_CAP + 64
 
 
 def general(node_loads, dest_owner, dest_elem, node_weight, mode_shapes, stiffness):
@@ -54,7 +55,11 @@
         "kem,ekr->mr", mode_shapes, elem_load, preferred_element_type=jnp.float32
     )
     scale = jnp.sqrt(jnp.float32(3.0 * rows * devices))
-    modal_force = lax.psum(partial_force, ("cfd", "struct"))
+    pieces = partial_force.reshape(devices, 1, -1)
+    pieces = lax.all_to_all(pieces, ("cfd", "struct"), split_axis=0, concat_axis=0, tiled=True)
+    piece = jnp.broadcast_to(jnp.sum(pieces, axis=0, keepdims=True), pieces.shape)
+    pieces = lax.all_to_all(piece, ("cfd", "struct"), split_axis=0, concat_axis=0, tiled=True)
+    modal_force = pieces.reshape(partial_force.shape)
     modal_amp = modal_force / (stiffness[:, None] * scale)
     amp_low = modal_amp.astype(jnp.bfloat16)
     elem_disp = jnp.einsum("kem,mr->ekr", mode_shapes, amp_low, preferred_element_type=jnp.float32)
@@ -72,6 +77,10 @@
     return jnp.dot(a, b, preferred_element_type=F32)
 
 
+def mm_nt(a, b):
+    return lax.dot_general(a, b, (((1,), (1,)), ((), ())), preferred_element_type=F32)
+
+
 def iota(shape, dim):
     return lax.broadcasted_iota(I32, shape, dim)
 
@@ -84,6 +93,11 @@
     low = iota(tail.shape, 1) < 64
     zero = jnp.zeros_like(tail)
     return jnp.concatenate([jnp.where(low, tail, zero), jnp.where(low, zero, tail)], axis=0)
+
+
+def unpack(block):
+    head = jnp.concatenate([block[0:CLASS_CAP], jnp.zeros((128 - CLASS_CAP, 128), BF16)], axis=0)
+    return jnp.concatenate([head, split_halves(block[CLASS_CAP:BLOCK])], axis=1)
 
 
 def fused_kernel(
@@ -91,24 +105,26 @@
     owner_ref, elem_ref, weight_ref, loads_ref, stiff_ref, mode_ref,
     out_ref, amp_ref,
     rows_ref, slot_ref, poison_ref, send1, keys_out, recv1, keys_in, acc, send2, recv2,
-    mode_v, force, piece_out, piece_in, ring_out, ring_in, total_in,
-    send3, recv3, disp, send4, recv4, slot_col, weight_col,
-    s1, r1, k1, q1, s2, r2, sa, ra, sb, rb, sc, rc, s3, r3, s4, r4, mode_sem,
+    mode_v, force, piece_out, piece_in, col_out, col_in, ring_out, ring_in, total_in,
+    send3, recv3, disp, send4, recv4, acc_t,
+    s1, r1, k1, q1, s2, r2, sa, ra, sy, ry, sb, rb, sc, rc, s3, r3, s4, r4, mode_sem,
 ):
     nz = n // ny
     me = lax.axis_index("cfd")
     st = lax.axis_index("struct")
     my_y, my_z = me // nz, lax.rem(me, nz)
-    my_q = my_y * ns + st
-    group = ny * ns
-    count = rows_ref.shape[0]
+    count = rows_ref.shape[1]
 
     def cfd_peer(t):
         return lax.rem(me + t, n)
 
-    def plane_peer(t):
-        q = lax.rem(my_q + t, group)
-        return q, ((q // ns) * nz + my_z, lax.rem(q, ns))
+    def struct_peer(t):
+        q = lax.rem(st + t, ns)
+        return q, (me, q)
+
+    def y_peer(t):
+        y = lax.rem(my_y + t, ny)
+        return y, (y * nz + my_z, st)
 
     def z_peer(t):
         z = lax.rem(my_z + t, nz)
@@ -120,20 +136,19 @@
         pl.semaphore_signal(barrier, inc=1, device_id=(cfd_peer(t), st), device_id_type=MESH)
         return 0
 
-    def greet_plane(t, _):
-        other = lax.rem(st + 1 + lax.rem(t, ns - 1), ns)
-        pl.semaphore_signal(
-            barrier, inc=1, device_id=(t // (ns - 1) * nz + my_z, other), device_id_type=MESH)
+    def greet_struct(t, _):
+        _, dev = struct_peer(t)
+        pl.semaphore_signal(barrier, inc=1, device_id=dev, device_id_type=MESH)
         return 0
 
     lax.fori_loop(1, n, greet_cfd, 0)
-    lax.fori_loop(0, ny * (ns - 1), greet_plane, 0)
+    lax.fori_loop(1, ns, greet_struct, 0)
     mode_copy = pltpu.make_async_copy(mode_ref, mode_v, mode_sem)
     mode_copy.start()
 
     owner = owner_ref[...]
     elem = elem_ref[...]
-    cls = lax.rem(elem // 64 + owner, n)
+    cls = ((elem >> 6) + owner) & (n - 1)
     upper = (iota((256, 256), 0) < iota((256, 256), 1)).astype(BF16)
     base = jnp.zeros((n, 1), F32)
     for q in range(count // 256):
@@ -142,22 +157,18 @@
         hit_f = hit.astype(F32)
         before = mm(hit_f.astype(BF16), upper) + base
         rank = jnp.sum(jnp.where(hit, before, 0.0), axis=0, keepdims=True).astype(I32)
-        slot_ref[:, 256 * q : 256 * q + 256] = jnp.where(rank < CLASS_CAP, part * CLASS_CAP + rank, -1)
+        slot_ref[:, 256 * q : 256 * q + 256] = jnp.where(rank < CLASS_CAP, part * 128 + rank, -1)
         base = base + jnp.sum(hit_f, axis=1, keepdims=True)
     most = jnp.max(base, axis=0, keepdims=True)
     poison_ref[...] = jnp.broadcast_to(jnp.where(most > CLASS_CAP, jnp.nan, 0.0), (8, 128))
 
-    for q in range(count // 128):
-        cols = slice(128 * q, 128 * q + 128)
-        sub = iota((128, 128), 0)
-        own = jnp.broadcast_to((owner[:, cols] + 1).astype(F32), (128, 128))
-        low = jnp.broadcast_to(lax.rem(elem[:, cols], 64).astype(F32), (128, 128))
-        meta = jnp.transpose(jnp.where(sub == 64, own, jnp.where(sub == 65, low, 0.0)))
-        rows_ref[cols, 0:128] = loads_ref[cols, 0:128]
-        tail = jnp.concatenate([loads_ref[cols, 128:192], jnp.zeros((128, 64), BF16)], axis=1)
-        rows_ref[cols, 128:256] = tail + meta.astype(BF16)
-
-    pl.semaphore_wait(barrier, n - 1 + group - ny)
+    sub = iota((64, count), 0)
+    own = jnp.broadcast_to(owner + 1, (64, count))
+    low_elem = jnp.broadcast_to(elem & 63, (64, count))
+    rows_ref[0:192, :] = loads_ref[...]
+    rows_ref[192:256, :] = jnp.where(sub == 0, own, jnp.where(sub == 1, low_elem, 0)).astype(F32).astype(BF16)
+
+    pl.semaphore_wait(barrier, n - 1 + ns - 1)
 
     def hop1(peer, src):
         return pltpu.make_async_remote_copy(
@@ -170,13 +181,13 @@
             device_id=(peer, st), device_id_type=MESH)
 
     def build(c):
-        slots = jnp.broadcast_to(slot_ref[...] - c * CLASS_CAP, (128, count))
+        slots = jnp.broadcast_to(slot_ref[...] - c * 128, (128, count))
         pick = (slots == iota((128, count), 0)).astype(BF16)
-        y = mm(pick, rows_ref[...])
+        y = mm_nt(pick, rows_ref[...])
         tail = y[:, 128:256]
-        send1[c, 0:128, :] = y[:, 0:128].astype(BF16)
+        send1[c, 0:CLASS_CAP, :] = y[0:CLASS_CAP, 0:128].astype(BF16)
         low = iota((64, 128), 1) < 64
-        send1[c, 128:192, :] = jnp.where(low, tail[0:64], pltpu.roll(tail[64:128], 64, 1)).astype(BF16)
+        send1[c, CLASS_CAP:BLOCK, :] = jnp.where(low, tail[0:64], pltpu.roll(tail[64:128], 64, 1)).astype(BF16)
         turned = jnp.transpose(tail)
         keys_out[c] = (turned[64:65] * 64.0 + turned[65:66] - 64.0).astype(I32)
 
@@ -206,7 +217,7 @@
                 hop1_keys(src, src).wait_recv()
 
             keys.append(keys_in[src])
-            parts.append(jnp.concatenate([recv1[src, 0:128, :], split_halves(recv1[src, 128:192, :])], axis=1))
+            parts.append(unpack(recv1[src]))
         keys = jnp.concatenate(keys, axis=1)
         parts = jnp.concatenate(parts, axis=0)
 
@@ -243,11 +254,6 @@
     lax.fori_loop(1, n, start2, 0)
     pack2(me)
     recv2[me] = send2[me]
-
-    for q in range(count // 128):
-        cols = slice(128 * q, 128 * q + 128)
-        slot_col[cols, :] = column(slot_ref[:, cols].astype(F32)).astype(I32)
-        weight_col[cols, :] = column(weight_ref[:, cols])
 
     mode_copy.wait()
     force[...] = jnp.zeros_like(force)
@@ -279,82 +285,57 @@
 
     lax.fori_loop(0, n // 4, project, 0)
 
-    rt = force.shape[0] // 8
-    ct = force.shape[1] // 128
-    for p in range(rt * ct):
-        i, j = p // ct, p % ct
-        piece_out[p] = force[8 * i : 8 * i + 8, 128 * j : 128 * j + 128] + poison_ref[...]
+    for p in range(ns):
+        piece_out[p] = force[8 * p : 8 * p + 8, :] + poison_ref[0:8, 0:1]
 
     def hop_a(q, dev, src):
         return pltpu.make_async_remote_copy(
             src_ref=piece_out.at[q], dst_ref=piece_in.at[src], send_sem=sa.at[q], recv_sem=ra.at[src],
             device_id=dev, device_id_type=MESH)
 
-    def start_a(t, _):
-        q, dev = plane_peer(t)
-        hop_a(q, dev, my_q).start()
-        return 0
-
-    lax.fori_loop(1, group, start_a, 0)
-    piece_in[my_q] = piece_out[my_q]
-
-    def wait_a(t, _):
-        q, dev = plane_peer(group - t)
-        hop_a(q, dev, q).wait_recv()
-        return 0
-
-    lax.fori_loop(1, group, wait_a, 0)
-    ring_out[...] = jnp.sum(piece_in[...], axis=0)
+    def hop_y(y, dev, src):
+        return pltpu.make_async_remote_copy(
+            src_ref=col_out, dst_ref=col_in.at[src], send_sem=sy.at[y], recv_sem=ry.at[src],
+            device_id=dev, device_id_type=MESH)
 
     def hop_b(z, dev, src):
         return pltpu.make_async_remote_copy(
             src_ref=ring_out, dst_ref=ring_in.at[src], send_sem=sb.at[z], recv_sem=rb.at[src],
             device_id=dev, device_id_type=MESH)
 
-    def start_b(t, _):
-        z, dev = z_peer(t)
-        hop_b(z, dev, my_z).start()
-        return 0
-
-    lax.fori_loop(1, nz, start_b, 0)
+    def hop_c(q, dev, piece):
+        return pltpu.make_async_remote_copy(
+            src_ref=total_in.at[piece], dst_ref=total_in.at[piece], send_sem=sc.at[q], recv_sem=rc.at[piece],
+            device_id=dev, device_id_type=MESH)
+
+    def phase(hop, peer_of, size, mine):
+        for t in range(1, size):
+            k, dev = peer_of(t)
+            hop(k, dev, mine).start()
+
+    def arrive(hop, peer_of, size):
+        for t in range(1, size):
+            k, dev = peer_of(size - t)
+            hop(k, dev, k).wait_recv()
+
+    phase(hop_a, struct_peer, ns, st)
+    piece_in[st] = piece_out[st]
+    arrive(hop_a, struct_peer, ns)
+    col_out[...] = jnp.sum(piece_in[...], axis=0)
+    phase(hop_y, y_peer, ny, my_y)
+    col_in[my_y] = col_out[...]
+    arrive(hop_y, y_peer, ny)
+    ring_out[...] = jnp.sum(col_in[...], axis=0)
+    phase(hop_b, z_peer, nz, my_z)
     ring_in[my_z] = ring_out[...]
-
-    def wait_b(t, _):
-        z, dev = z_peer(nz - t)
-        hop_b(z, dev, z).wait_recv()
-        return 0
-
-    lax.fori_loop(1, nz, wait_b, 0)
-    total_in[my_q] = jnp.sum(ring_in[...], axis=0)
-
-    def hop_c(q, dev):
-        return pltpu.make_async_remote_copy(
-            src_ref=total_in.at[my_q], dst_ref=total_in.at[my_q], send_sem=sc.at[q], recv_sem=rc.at[my_q],
-            device_id=dev, device_id_type=MESH)
-
-    def got_c(q, dev):
-        return pltpu.make_async_remote_copy(
-            src_ref=total_in.at[q], dst_ref=total_in.at[q], send_sem=sc.at[q], recv_sem=rc.at[q],
-            device_id=dev, device_id_type=MESH)
-
-    def start_c(t, _):
-        q, dev = plane_peer(t)
-        hop_c(q, dev).start()
-        return 0
-
-    lax.fori_loop(1, group, start_c, 0)
-
-    def wait_c(t, _):
-        q, dev = plane_peer(group - t)
-        got_c(q, dev).wait_recv()
-        return 0
-
-    lax.fori_loop(1, group, wait_c, 0)
-    whole = jnp.concatenate(
-        [jnp.concatenate([total_in[i * ct + j] for j in range(ct)], axis=1) for i in range(rt)], axis=0)
+    arrive(hop_b, z_peer, nz)
+    total_in[st] = jnp.sum(ring_in[...], axis=0)
+    phase(hop_c, struct_peer, ns, st)
+    arrive(hop_c, struct_peer, ns)
+    whole = jnp.concatenate([total_in[p] for p in range(ns)], axis=0)
     amp_t = whole / (stiff_ref[...] * nodes_scale)
+    amp_ref[...] = amp_t
     amp = jnp.transpose(jnp.concatenate([amp_t, amp_t], axis=0))
-    amp_ref[...] = amp[:, 0:64]
     both = amp.astype(BF16)
     low = iota(amp.shape, 1) < 64
     left = jnp.where(low, amp, 0.0).astype(BF16)
@@ -416,8 +397,8 @@
             [(keys - 128 * q == lane).astype(BF16) for q in range(disp.shape[0] // 128)], axis=1)
         y = mm(pick, disp[...])
         keep = iota((64, 128), 1) < 64
-        send4[src, 0:128, :] = y[:, 0:128].astype(BF16)
-        send4[src, 128:192, :] = jnp.where(keep, y[0:64, 128:256], y[64:128, 128:256]).astype(BF16)
+        send4[src, 0:CLASS_CAP, :] = y[0:CLASS_CAP, 0:128].astype(BF16)
+        send4[src, CLASS_CAP:BLOCK, :] = jnp.where(keep, y[0:64, 128:256], y[64:128, 128:256]).astype(BF16)
 
     def start4(t, _):
         src = cfd_peer(t)
@@ -429,7 +410,7 @@
     gather(me)
     recv4[me] = send4[me]
 
-    acc[...] = jnp.zeros_like(acc)
+    acc_t[...] = jnp.zeros_like(acc_t)
 
     def place(g, _):
         parts, firsts = [], []
@@ -441,33 +422,23 @@
             def _():
                 hop4(src, src).wait_recv()
 
-            firsts.append(src * CLASS_CAP)
-            parts.append(jnp.concatenate([recv4[src, 0:128, :], split_halves(recv4[src, 128:192, :])], axis=1))
+            firsts.append(src * 128)
+            parts.append(unpack(recv4[src]))
         parts = jnp.concatenate(parts, axis=0)
-
-        def block(b, _):
-            at = pl.ds(pl.multiple_of(b * 256, 256), 256)
-            slots = slot_col[at, :]
-            lane = iota((256, 128), 1)
-            pick = jnp.concatenate([(slots - first == lane).astype(BF16) for first in firsts], axis=1)
-            acc[at, :] += mm(pick, parts)
-            return 0
-
-        lax.fori_loop(0, count // 256, block, 0)
+        parts = jnp.transpose(parts.astype(F32)).astype(BF16)
+        for b in range(count // 512):
+            at = slice(512 * b, 512 * b + 512)
+            slots = slot_ref[:, at]
+            sub = iota((128, 512), 0)
+            pick = jnp.concatenate(
+                [(jnp.broadcast_to(slots - first, (128, 512)) == sub).astype(BF16) for first in firsts], axis=0)
+            acc_t[:, at] += mm(parts, pick)
         return 0
 
     lax.fori_loop(0, n // 4, place, 0)
-
-    def finish(b, _):
-        at = pl.ds(pl.multiple_of(b * 256, 256), 256)
-        w = weight_col[at, :]
-        out_ref[at, 0:128] = (acc[at, 0:128] * w).astype(BF16)
-        tail = acc[at, 128:256]
-        tail = (tail + pltpu.roll(tail, 64, 1)) * w
-        out_ref[at, 128:192] = tail[:, 0:64].astype(BF16)
-        return 0
-
-    lax.fori_loop(0, count // 256, finish, 0)
+    weight = weight_ref[...]
+    out_ref[0:128, :] = (acc_t[0:128, :] * weight).astype(BF16)
+    out_ref[128:192, :] = ((acc_t[128:192, :] + acc_t[192:256, :]) * weight).astype(BF16)
 
     def sent(t, _):
         peer = cfd_peer(t)
@@ -480,20 +451,16 @@
 
     lax.fori_loop(1, n, sent, 0)
 
-    def sent_plane(t, _):
-        q, dev = plane_peer(t)
-        hop_a(q, dev, my_q).wait_send()
-        hop_c(q, dev).wait_send()
-        return 0
-
-    lax.fori_loop(1, group, sent_plane, 0)
-
-    def sent_z(t, _):
+    for t in range(1, ns):
+        q, dev = struct_peer(t)
+        hop_a(q, dev, st).wait_send()
+        hop_c(q, dev, st).wait_send()
+    for t in range(1, ny):
+        y, dev = y_peer(t)
+        hop_y(y, dev, my_y).wait_send()
+    for t in range(1, nz):
         z, dev = z_peer(t)
         hop_b(z, dev, my_z).wait_send()
-        return 0
-
-    lax.fori_loop(1, nz, sent_z, 0)
 
 
 def fast(node_loads, dest_owner, dest_elem, node_weight, mode_shapes, stiffness):
@@ -501,31 +468,31 @@
     n, ns = lax.axis_size("cfd"), lax.axis_size("struct")
     ny = 4
     nz = n // ny
-    group = ny * ns
     comps, elems, modes = mode_shapes.shape
     scale = float(np.sqrt(np.float32(3.0 * rows * n * ns)))
     vmem = pl.BlockSpec(memory_space=pltpu.VMEM)
     dma = pltpu.SemaphoreType.DMA
-    pair = (n, 192, 128)
+    pair = (n, BLOCK, 128)
     dense = (n, 96, 128)
-    return pl.pallas_call(
+    piece = (64 // ns, modes)
+    out_t, amp_t = pl.pallas_call(
         functools.partial(fused_kernel, n, ny, ns, scale),
-        out_shape=(jax.ShapeDtypeStruct((rows, width), BF16), jax.ShapeDtypeStruct((modes, 64), F32)),
+        out_shape=(jax.ShapeDtypeStruct((width, rows), BF16), jax.ShapeDtypeStruct((64, modes), F32)),
         in_specs=[vmem] * 5 + [pl.BlockSpec(memory_space=pl.ANY)],
         out_specs=(vmem, vmem),
         scratch_shapes=[
-            pltpu.VMEM((rows, 256), BF16), pltpu.VMEM((1, rows), I32), pltpu.VMEM((8, 128), F32),
+            pltpu.VMEM((256, rows), BF16), pltpu.VMEM((1, rows), I32), pltpu.VMEM((8, 128), F32),
             pltpu.VMEM(pair, BF16), pltpu.VMEM((n, 1, 128), I32),
             pltpu.VMEM(pair, BF16), pltpu.VMEM((n, 1, 128), I32),
-            pltpu.VMEM((rows, 256), F32), pltpu.VMEM(dense, BF16), pltpu.VMEM(dense, BF16),
+            pltpu.VMEM((elems, 256), F32), pltpu.VMEM(dense, BF16), pltpu.VMEM(dense, BF16),
             pltpu.VMEM(mode_shapes.shape, BF16), pltpu.VMEM((64, modes), F32),
-            pltpu.VMEM((group, 8, 128), F32), pltpu.VMEM((group, 8, 128), F32),
-            pltpu.VMEM((8, 128), F32), pltpu.VMEM((nz, 8, 128), F32), pltpu.VMEM((group, 8, 128), F32),
+            pltpu.VMEM((ns,) + piece, F32), pltpu.VMEM((ns,) + piece, F32),
+            pltpu.VMEM(piece, F32), pltpu.VMEM((ny,) + piece, F32),
+            pltpu.VMEM(piece, F32), pltpu.VMEM((nz,) + piece, F32), pltpu.VMEM((ns,) + piece, F32),
             pltpu.VMEM(dense, BF16), pltpu.VMEM(dense, BF16), pltpu.VMEM((elems, 256), BF16),
-            pltpu.VMEM(pair, BF16), pltpu.VMEM(pair, BF16),
-            pltpu.VMEM((rows, 128), I32), pltpu.VMEM((rows, 128), F32),
+            pltpu.VMEM(pair, BF16), pltpu.VMEM(pair, BF16), pltpu.VMEM((256, rows), F32),
             dma((n,)), dma((n,)), dma((n,)), dma((n,)), dma((n,)), dma((n,)),
-            dma((group,)), dma((group,)), dma((nz,)), dma((nz,)), dma((group,)), dma((group,)),
+            dma((ns,)), dma((ns,)), dma((ny,)), dma((ny,)), dma((nz,)), dma((nz,)), dma((ns,)), dma((ns,)),
             dma((n,)), dma((n,)), dma((n,)), dma((n,)), dma(()),
         ],
         compiler_params=pltpu.CompilerParams(
@@ -533,8 +500,9 @@
         cost_estimate=pl.CostEstimate(flops=30_000_000_000, bytes_accessed=10_000_000, transcendentals=0),
     )(
         dest_owner.reshape(1, rows), dest_elem.reshape(1, rows), node_weight.reshape(1, rows),
-        node_loads, stiffness.reshape(1, modes), mode_shapes,
-    )
+        node_loads.T, stiffness.reshape(1, modes), mode_shapes,
+    )
+    return out_t.T, amp_t.T
 
 
 def per_device(*args):

time: 175 us -> 152 us (0.87)
  between operations: 15.3 us -> 1.99 us
  Pallas kernels: 155 us -> 148 us
  local copies, waits for them, and re-layouts: 4.91 us -> 2.06 us
    pallas_call x1, Pallas kernels: 155 us -> 148 us  [fast(): pl.pallas_call(functools.partial(fused_kernel, n, ny, ns, scale), out_sha...]
where the time goes in v2:
time: 152 us
  Pallas kernels  148 us (97%)
  local copies, waits for them, and re-layouts  2.06 us (1%)
  between operations  1.99 us (1%)
    pallas_call x1, Pallas kernels, fast(): pl.pallas_call(functools.partial(fused_kernel, n, ny, ns, scale), out_sha...  148 us

profile of v2, /device:TPU:32, one launch (start us, length us, event | category | flops | bytes accessed | tf_op | source)
XLA Modules:
  0.0 151.9 jit_solution(14781769433341910253)
XLA Ops:
  0.6 0.0 copy-start.1
  0.6 0.0 copy-start.2
  0.6 0.0 copy-start.4
  0.7 147.6 %shard_map.81 = (bf16[192,2048]{1,0:T(8,128)(2,1)S(1)}, f32[64,512]{1,0:T(8,128)S(1)}) custom-call(s32[1,2048]{1,0:T(1,128)} %bitcast.76, s32[1,2048]{1,0:T(1,128)} %bitcast.84, f32[1,2048]{1,0:T(1,128)} %bitcast.82, bf16[192,2048]{1,0:T(8,128)(2,1)} %bitcast.68, f32[1,512]{1,0:T(1,128)} %bitcast.83, bf16[3,2048,512]{2,1,0:T(8,128)(2,1)} %mode_ref.1), custom_call_target="tpu_custom_call" | custom-call | flops 30000001024 | bytes 10000000 | tf_op jit(solution)/shard_map/pallas_call | solution.py:478
  148.3 0.5 slice.16
  150.1 0.0 copy-done.1
  150.1 0.0 copy-done.2
  150.1 0.0 copy-done.4
  150.1 0.2 conditional.1
  150.4 0.9 copy.93
  151.2 0.7 copy.94
Async XLA Ops:
  0.6 149.5 %copy-start.1 = (bf16[2048,192]{0,1:T(8,128)(2,1)S(1)}, bf16[2048,192]{0,1:T(8,128)(2,1)}, u32[]{:S(2)}) copy-start(bf16[2048,192]{0,1:T(8,128)(2,1)} %param.10) | copy-start | bytes 2359300
  0.6 149.5 %copy-start.2 = (s32[2048,1]{0,1:T(1,128)S(1)}, s32[2048,1]{0,1:T(1,128)}, u32[]{:S(2)}) copy-start(s32[2048,1]{0,1:T(1,128)} %param.11) | copy-start | bytes 24580
  0.6 149.5 %copy-start.4 = (f32[512]{0:T(512)S(1)}, f32[512]{0:T(512)}, u32[]{:S(2)}) copy-start(f32[512]{0:T(512)} %param.15) | copy-start | bytes 6148

commit v3 on v2

--- a/solution.py
+++ b/solution.py
@@ -12,7 +12,6 @@
 MESH = pl.DeviceIdType.MESH
 BF16, F32, I32 = jnp.bfloat16, jnp.float32, jnp.int32
 CLASS_CAP = 112
-BLOCK = CLASS_CAP + 64
 
 
 def general(node_loads, dest_owner, dest_elem, node_weight, mode_shapes, stiffness):
@@ -85,6 +84,15 @@
     return lax.broadcasted_iota(I32, shape, dim)
 
 
+def chosen(row, value, tall):
+    few = (jnp.broadcast_to(row, (16, row.shape[1])) == value).astype(F32).astype(BF16)
+    return jnp.concatenate([few] * (tall // 16), axis=0)
+
+
+def one_hot(row, tall):
+    return (jnp.broadcast_to(row, (tall, row.shape[1])) == iota((tall, row.shape[1]), 0)).astype(F32).astype(BF16)
+
+
 def column(row):
     return jnp.transpose(jnp.broadcast_to(row, (128, 128)))
 
@@ -95,19 +103,20 @@
     return jnp.concatenate([jnp.where(low, tail, zero), jnp.where(low, zero, tail)], axis=0)
 
 
-def unpack(block):
-    head = jnp.concatenate([block[0:CLASS_CAP], jnp.zeros((128 - CLASS_CAP, 128), BF16)], axis=0)
-    return jnp.concatenate([head, split_halves(block[CLASS_CAP:BLOCK])], axis=1)
+def padded(head):
+    return jnp.concatenate([head, jnp.zeros((128 - CLASS_CAP, 128), BF16)], axis=0)
 
 
 def fused_kernel(
     n, ny, ns, nodes_scale,
     owner_ref, elem_ref, weight_ref, loads_ref, stiff_ref, mode_ref,
     out_ref, amp_ref,
-    rows_ref, slot_ref, poison_ref, send1, keys_out, recv1, keys_in, acc, send2, recv2,
-    mode_v, force, piece_out, piece_in, col_out, col_in, ring_out, ring_in, total_in,
-    send3, recv3, disp, send4, recv4, acc_t,
-    s1, r1, k1, q1, s2, r2, sa, ra, sy, ry, sb, rb, sc, rc, s3, r3, s4, r4, mode_sem,
+    rows_ref, slot_ref, poison_ref, keys_out, keys_in, acc, acc_t,
+    send1, recv1, send2, recv2, send3, recv3, send4, recv4,
+    send1t, recv1t, send2t, recv2t, send3t, recv3t, send4t, recv4t,
+    mode_v, force, piece_out, piece_in, col_out, col_in, ring_out, ring_in, total_in, disp, picks, base_ref,
+    s1, r1, s2, r2, s3, r3, s4, r4, s1t, r1t, s2t, r2t, s3t, r3t, s4t, r4t,
+    k1, q1, sa, ra, sy, ry, sb, rb, sc, rc, mode_sem,
 ):
     nz = n // ny
     me = lax.axis_index("cfd")
@@ -125,6 +134,20 @@
     def y_peer(t):
         y = lax.rem(my_y + t, ny)
         return y, (y * nz + my_z, st)
+
+    def hop_of(out, into, send, recv):
+        def hop(peer, src):
+            return pltpu.make_async_remote_copy(
+                src_ref=out.at[peer], dst_ref=into.at[src], send_sem=send.at[peer], recv_sem=recv.at[src],
+                device_id=(peer, st), device_id_type=MESH)
+
+        return hop
+
+    hop1, hop1t = hop_of(send1, recv1, s1, r1), hop_of(send1t, recv1t, s1t, r1t)
+    hop2, hop2t = hop_of(send2, recv2, s2, r2), hop_of(send2t, recv2t, s2t, r2t)
+    hop3, hop3t = hop_of(send3, recv3, s3, r3), hop_of(send3t, recv3t, s3t, r3t)
+    hop4, hop4t = hop_of(send4, recv4, s4, r4), hop_of(send4t, recv4t, s4t, r4t)
+    hop1_keys = hop_of(keys_out, keys_in, k1, q1)
 
     def z_peer(t):
         z = lax.rem(my_z + t, nz)
@@ -168,44 +191,43 @@
     rows_ref[0:192, :] = loads_ref[...]
     rows_ref[192:256, :] = jnp.where(sub == 0, own, jnp.where(sub == 1, low_elem, 0)).astype(F32).astype(BF16)
 
+    base_ref[...] = one_hot(slot_ref[...] & 127, 128)
     pl.semaphore_wait(barrier, n - 1 + ns - 1)
 
-    def hop1(peer, src):
-        return pltpu.make_async_remote_copy(
-            src_ref=send1.at[peer], dst_ref=recv1.at[src], send_sem=s1.at[peer], recv_sem=r1.at[src],
-            device_id=(peer, st), device_id_type=MESH)
-
-    def hop1_keys(peer, src):
-        return pltpu.make_async_remote_copy(
-            src_ref=keys_out.at[peer], dst_ref=keys_in.at[src], send_sem=k1.at[peer], recv_sem=q1.at[src],
-            device_id=(peer, st), device_id_type=MESH)
-
-    def build(c):
-        slots = jnp.broadcast_to(slot_ref[...] - c * 128, (128, count))
-        pick = (slots == iota((128, count), 0)).astype(BF16)
-        y = mm_nt(pick, rows_ref[...])
-        tail = y[:, 128:256]
-        send1[c, 0:CLASS_CAP, :] = y[0:CLASS_CAP, 0:128].astype(BF16)
+    def build(g, _):
+        classes = [cfd_peer(g * 4 + u) for u in range(4)]
+        wanted = slot_ref[...] >> 7
+        pick = jnp.concatenate([base_ref[...] * chosen(wanted, c, 128) for c in classes], axis=0)
+        y4 = mm_nt(pick, rows_ref[...])
         low = iota((64, 128), 1) < 64
-        send1[c, CLASS_CAP:BLOCK, :] = jnp.where(low, tail[0:64], pltpu.roll(tail[64:128], 64, 1)).astype(BF16)
-        turned = jnp.transpose(tail)
-        keys_out[c] = (turned[64:65] * 64.0 + turned[65:66] - 64.0).astype(I32)
-
-    def start1(t, _):
-        c = cfd_peer(t)
-        build(c)
-        hop1(c, me).start()
-        hop1_keys(c, me).start()
-        return 0
-
-    lax.fori_loop(1, n, start1, 0)
-    build(me)
+        for u, c in enumerate(classes):
+            y = y4[128 * u : 128 * u + 128]
+            tail = y[:, 128:256]
+            send1[c] = y[0:CLASS_CAP, 0:128].astype(BF16)
+            send1t[c] = jnp.where(low, tail[0:64], pltpu.roll(tail[64:128], 64, 1)).astype(BF16)
+            turned = jnp.transpose(tail)
+            keys_out[c] = (turned[64:65] * 64.0 + turned[65:66] - 64.0).astype(I32)
+
+            @pl.when(g * 4 + u > 0)
+            def _():
+                hop1(c, me).start()
+                hop1_keys(c, me).start()
+
+        return 0
+
+    def start1_tail(t, _):
+        hop1t(cfd_peer(t), me).start()
+        return 0
+
+    lax.fori_loop(0, n // 4, build, 0)
+    lax.fori_loop(1, n, start1_tail, 0)
     recv1[me] = send1[me]
+    recv1t[me] = send1t[me]
     keys_in[me] = keys_out[me]
 
     acc[...] = jnp.zeros_like(acc)
 
-    def combine(g, _):
+    def combine(g, hops, part, first):
         keys, parts = [], []
         for u in range(4):
             t = g * 4 + u
@@ -213,37 +235,29 @@
 
             @pl.when(t > 0)
             def _():
-                hop1(src, src).wait_recv()
-                hop1_keys(src, src).wait_recv()
+                for hop in hops:
+                    hop(src, src).wait_recv()
 
             keys.append(keys_in[src])
-            parts.append(unpack(recv1[src]))
+            parts.append(part(src))
         keys = jnp.concatenate(keys, axis=1)
         parts = jnp.concatenate(parts, axis=0)
-
-        def block(b, _):
-            at = pl.ds(pl.multiple_of(b * 256, 256), 256)
-            hit = jnp.broadcast_to(keys - b * 256, (256, 512)) == iota((256, 512), 0)
-            acc[at, :] += mm(hit.astype(BF16), parts)
-            return 0
-
-        lax.fori_loop(0, acc.shape[0] // 256, block, 0)
-        return 0
-
-    lax.fori_loop(0, n // 4, combine, 0)
-
-    def hop2(peer, src):
-        return pltpu.make_async_remote_copy(
-            src_ref=send2.at[peer], dst_ref=recv2.at[src], send_sem=s2.at[peer], recv_sem=r2.at[src],
-            device_id=(peer, st), device_id_type=MESH)
+        low_hit = one_hot(keys & 255, 256)
+
+        hit = jnp.concatenate([low_hit * chosen(keys >> 8, b, 256) for b in range(acc.shape[0] // 256)], axis=0)
+        acc[:, first : first + 128] += mm(hit, parts)
+        return 0
 
     def pack2(d):
         at = pl.ds(pl.multiple_of(d * 64, 64), 64)
-        send2[d, 0:64, :] = acc[at, 0:128].astype(BF16)
+        send2[d] = acc[at, 0:128].astype(BF16)
+
+    def pack2_tail(d):
+        at = pl.ds(pl.multiple_of(d * 64, 64), 64)
         tail = acc[at, 128:256]
         tail = tail + pltpu.roll(tail, 64, 1)
         low = iota((32, 128), 1) < 64
-        send2[d, 64:96, :] = jnp.where(low, tail[0:32], tail[32:64]).astype(BF16)
+        send2t[d] = jnp.where(low, tail[0:32], tail[32:64]).astype(BF16)
 
     def start2(t, _):
         d = cfd_peer(t)
@@ -251,39 +265,57 @@
         hop2(d, me).start()
         return 0
 
+    def start2_tail(t, _):
+        d = cfd_peer(t)
+        pack2_tail(d)
+        hop2t(d, me).start()
+        return 0
+
+    lax.fori_loop(0, n // 4, lambda g, _: combine(g, (hop1, hop1_keys), lambda src: padded(recv1[src]), 0), 0)
     lax.fori_loop(1, n, start2, 0)
     pack2(me)
     recv2[me] = send2[me]
+    lax.fori_loop(0, n // 4, lambda g, _: combine(g, (hop1t,), lambda src: split_halves(recv1t[src]), 128), 0)
+    lax.fori_loop(1, n, start2_tail, 0)
+    pack2_tail(me)
+    recv2t[me] = send2t[me]
 
     mode_copy.wait()
     force[...] = jnp.zeros_like(force)
 
-    def project(g, _):
+    def project(g, hop, part):
         parts = []
         for u in range(4):
-            b = g * 4 + u
-            blk = n - 1 - b
+            blk = n - 1 - (g * 4 + u)
             src = lax.rem(me + blk, n)
 
             @pl.when(blk > 0)
             def _():
-                hop2(src, src).wait_recv()
-
-            tail = recv2[src, 64:96, :]
-            low = iota((32, 128), 1) < 64
-            zero = jnp.zeros_like(tail)
-            tail = jnp.concatenate([jnp.where(low, tail, zero), jnp.where(low, zero, tail)], axis=0)
-            parts.append(jnp.concatenate([recv2[src, 0:64, :], tail], axis=1))
+                hop(src, src).wait_recv()
+
+            parts.append(part(src))
         load = jnp.concatenate(parts[::-1], axis=0)
-        load = jnp.transpose(load.astype(F32)).astype(BF16)
-        at = pl.ds(pl.multiple_of((n // 4 - 1 - g) * 256, 256), 256)
-        f0 = mm(load[0:64], mode_v[0, at, :])
-        f1 = mm(load[64:128], mode_v[1, at, :])
-        f2 = mm(load[128:256], mode_v[2, at, :])
-        force[...] += f0 + f1 + f2[0:64] + f2[64:128]
-        return 0
-
-    lax.fori_loop(0, n // 4, project, 0)
+        return jnp.transpose(load.astype(F32)).astype(BF16), pl.ds(pl.multiple_of((n // 4 - 1 - g) * 256, 256), 256)
+
+    def project_head(g, _):
+        load, at = project(g, hop2, lambda src: recv2[src])
+        force[...] += mm(load[0:64], mode_v[0, at, :]) + mm(load[64:128], mode_v[1, at, :])
+        return 0
+
+    def tail_of(src):
+        tail = recv2t[src]
+        low = iota((32, 128), 1) < 64
+        zero = jnp.zeros_like(tail)
+        return jnp.concatenate([jnp.where(low, tail, zero), jnp.where(low, zero, tail)], axis=0)
+
+    def project_tail(g, _):
+        load, at = project(g, hop2t, tail_of)
+        f2 = mm(load, mode_v[2, at, :])
+        force[...] += f2[0:64] + f2[64:128]
+        return 0
+
+    lax.fori_loop(0, n // 4, project_head, 0)
+    lax.fori_loop(0, n // 4, project_tail, 0)
 
     for p in range(ns):
         piece_out[p] = force[8 * p : 8 * p + 8, :] + poison_ref[0:8, 0:1]
@@ -341,22 +373,13 @@
     left = jnp.where(low, amp, 0.0).astype(BF16)
     right = jnp.where(low, 0.0, amp).astype(BF16)
 
-    def hop3(peer, src):
-        return pltpu.make_async_remote_copy(
-            src_ref=send3.at[peer], dst_ref=recv3.at[src], send_sem=s3.at[peer], recv_sem=r3.at[src],
-            device_id=(peer, st), device_id_type=MESH)
-
     def expand(g, _):
         at = pl.ds(pl.multiple_of(g * 256, 256), 256)
         d01 = (mm(mode_v[0, at, :], left) + mm(mode_v[1, at, :], right)).astype(BF16)
-        d2 = mm(mode_v[2, at, :], both)
         for u in range(4):
             b = g * 4 + u
             peer = cfd_peer(b)
-            send3[peer, 0:64, :] = d01[64 * u : 64 * u + 64]
-            keep = iota((32, 128), 1) < 64
-            send3[peer, 64:96, :] = jnp.where(
-                keep, d2[64 * u : 64 * u + 32], d2[64 * u + 32 : 64 * u + 64]).astype(BF16)
+            send3[peer] = d01[64 * u : 64 * u + 64]
 
             @pl.when(b > 0)
             def _():
@@ -364,8 +387,35 @@
 
         return 0
 
+    def expand_tail(g, _):
+        at = pl.ds(pl.multiple_of(g * 256, 256), 256)
+        d2 = mm(mode_v[2, at, :], both)
+        keep = iota((32, 128), 1) < 64
+        for u in range(4):
+            b = g * 4 + u
+            peer = cfd_peer(b)
+            send3t[peer] = jnp.where(keep, d2[64 * u : 64 * u + 32], d2[64 * u + 32 : 64 * u + 64]).astype(BF16)
+
+            @pl.when(b > 0)
+            def _():
+                hop3t(peer, me).start()
+
+        return 0
+
     lax.fori_loop(0, n // 4, expand, 0)
+    lax.fori_loop(0, n // 4, expand_tail, 0)
     recv3[me] = send3[me]
+    recv3t[me] = send3t[me]
+
+    def choose(src, _):
+        keys = column(keys_in[src].astype(F32)).astype(I32)
+        low_hit = (keys & 127 == iota((128, 128), 1)).astype(F32).astype(BF16)
+        high = (keys >> 7).astype(F32).astype(BF16)
+        for q in range(disp.shape[0] // 128):
+            picks[src, :, 128 * q : 128 * q + 128] = jnp.where(high == q, low_hit, jnp.zeros_like(low_hit))
+        return 0
+
+    lax.fori_loop(0, n, choose, 0)
 
     def unpack3(t, _):
         src = lax.rem(me + n - t, n)
@@ -374,45 +424,60 @@
         def _():
             hop3(src, src).wait_recv()
 
+        disp[pl.ds(pl.multiple_of(src * 64, 64), 64), 0:128] = recv3[src]
+        return 0
+
+    def unpack3_tail(t, _):
+        src = lax.rem(me + n - t, n)
+
+        @pl.when(t > 0)
+        def _():
+            hop3t(src, src).wait_recv()
+
         at = pl.multiple_of(src * 64, 64)
-        disp[pl.ds(at, 64), 0:128] = recv3[src, 0:64, :]
-        tail = recv3[src, 64:96, :].astype(F32)
+        tail = recv3t[src].astype(F32)
         other = pltpu.roll(tail, 64, 1)
         keep = iota((32, 128), 1) < 64
         disp[pl.ds(at, 32), 128:256] = jnp.where(keep, tail, other).astype(BF16)
         disp[pl.ds(at + 32, 32), 128:256] = jnp.where(keep, other, tail).astype(BF16)
         return 0
 
+    def gather(g, _):
+        sources = [cfd_peer(g * 4 + u) for u in range(4)]
+        y4 = mm(jnp.concatenate([picks[src] for src in sources], axis=0), disp[:, 0:128])
+        for u, src in enumerate(sources):
+            send4[src] = y4[128 * u : 128 * u + CLASS_CAP].astype(BF16)
+
+            @pl.when(g * 4 + u > 0)
+            def _():
+                hop4(src, me).start()
+
+        return 0
+
+    def gather_tail(g, _):
+        sources = [cfd_peer(g * 4 + u) for u in range(4)]
+        y4 = mm(jnp.concatenate([picks[src] for src in sources], axis=0), disp[:, 128:256])
+        keep = iota((64, 128), 1) < 64
+        for u, src in enumerate(sources):
+            y = y4[128 * u : 128 * u + 128]
+            send4t[src] = jnp.where(keep, y[0:64], y[64:128]).astype(BF16)
+
+            @pl.when(g * 4 + u > 0)
+            def _():
+                hop4t(src, me).start()
+
+        return 0
+
     lax.fori_loop(0, n, unpack3, 0)
-
-    def hop4(peer, src):
-        return pltpu.make_async_remote_copy(
-            src_ref=send4.at[peer], dst_ref=recv4.at[src], send_sem=s4.at[peer], recv_sem=r4.at[src],
-            device_id=(peer, st), device_id_type=MESH)
-
-    def gather(src):
-        keys = column(keys_in[src].astype(F32)).astype(I32)
-        lane = iota((128, 128), 1)
-        pick = jnp.concatenate(
-            [(keys - 128 * q == lane).astype(BF16) for q in range(disp.shape[0] // 128)], axis=1)
-        y = mm(pick, disp[...])
-        keep = iota((64, 128), 1) < 64
-        send4[src, 0:CLASS_CAP, :] = y[0:CLASS_CAP, 0:128].astype(BF16)
-        send4[src, CLASS_CAP:BLOCK, :] = jnp.where(keep, y[0:64, 128:256], y[64:128, 128:256]).astype(BF16)
-
-    def start4(t, _):
-        src = cfd_peer(t)
-        gather(src)
-        hop4(src, me).start()
-        return 0
-
-    lax.fori_loop(1, n, start4, 0)
-    gather(me)
+    lax.fori_loop(0, n // 4, gather, 0)
     recv4[me] = send4[me]
+    lax.fori_loop(0, n, unpack3_tail, 0)
+    lax.fori_loop(0, n // 4, gather_tail, 0)
+    recv4t[me] = send4t[me]
 
     acc_t[...] = jnp.zeros_like(acc_t)
 
-    def place(g, _):
+    def place(g, hop, part, first_row):
         parts, firsts = [], []
         for u in range(4):
             t = g * 4 + u
@@ -420,33 +485,30 @@
 
             @pl.when(t > 0)
             def _():
-                hop4(src, src).wait_recv()
-
-            firsts.append(src * 128)
-            parts.append(unpack(recv4[src]))
+                hop(src, src).wait_recv()
+
+            firsts.append(src)
+            parts.append(part(src))
         parts = jnp.concatenate(parts, axis=0)
         parts = jnp.transpose(parts.astype(F32)).astype(BF16)
         for b in range(count // 512):
             at = slice(512 * b, 512 * b + 512)
-            slots = slot_ref[:, at]
-            sub = iota((128, 512), 0)
-            pick = jnp.concatenate(
-                [(jnp.broadcast_to(slots - first, (128, 512)) == sub).astype(BF16) for first in firsts], axis=0)
-            acc_t[:, at] += mm(parts, pick)
-        return 0
-
-    lax.fori_loop(0, n // 4, place, 0)
+            classes = slot_ref[:, at] >> 7
+            base = base_ref[:, at]
+            pick = jnp.concatenate([base * chosen(classes, first, 128) for first in firsts], axis=0)
+            acc_t[first_row : first_row + 128, at] += mm(parts, pick)
+        return 0
+
+    lax.fori_loop(0, n // 4, lambda g, _: place(g, hop4, lambda src: padded(recv4[src]), 0), 0)
+    lax.fori_loop(0, n // 4, lambda g, _: place(g, hop4t, lambda src: split_halves(recv4t[src]), 128), 0)
     weight = weight_ref[...]
     out_ref[0:128, :] = (acc_t[0:128, :] * weight).astype(BF16)
     out_ref[128:192, :] = ((acc_t[128:192, :] + acc_t[192:256, :]) * weight).astype(BF16)
 
     def sent(t, _):
         peer = cfd_peer(t)
-        hop1(peer, me).wait_send()
-        hop1_keys(peer, me).wait_send()
-        hop2(peer, me).wait_send()
-        hop3(peer, me).wait_send()
-        hop4(peer, me).wait_send()
+        for hop in (hop1, hop1t, hop1_keys, hop2, hop2t, hop3, hop3t, hop4, hop4t):
+            hop(peer, me).wait_send()
         return 0
 
     lax.fori_loop(1, n, sent, 0)
@@ -472,8 +534,8 @@
     scale = float(np.sqrt(np.float32(3.0 * rows * n * ns)))
     vmem = pl.BlockSpec(memory_space=pltpu.VMEM)
     dma = pltpu.SemaphoreType.DMA
-    pair = (n, BLOCK, 128)
-    dense = (n, 96, 128)
+    head, tail = (n, CLASS_CAP, 128), (n, 64, 128)
+    dense, dense_tail = (n, 64, 128), (n, 32, 128)
     piece = (64 // ns, modes)
     out_t, amp_t = pl.pallas_call(
         functools.partial(fused_kernel, n, ny, ns, scale),
@@ -482,18 +544,18 @@
         out_specs=(vmem, vmem),
         scratch_shapes=[
             pltpu.VMEM((256, rows), BF16), pltpu.VMEM((1, rows), I32), pltpu.VMEM((8, 128), F32),
-            pltpu.VMEM(pair, BF16), pltpu.VMEM((n, 1, 128), I32),
-            pltpu.VMEM(pair, BF16), pltpu.VMEM((n, 1, 128), I32),
-            pltpu.VMEM((elems, 256), F32), pltpu.VMEM(dense, BF16), pltpu.VMEM(dense, BF16),
+            pltpu.VMEM((n, 1, 128), I32), pltpu.VMEM((n, 1, 128), I32),
+            pltpu.VMEM((elems, 256), F32), pltpu.VMEM((256, rows), F32),
+            *(pltpu.VMEM(v, BF16) for v in (head, head, dense, dense, dense, dense, head, head)),
+            *(pltpu.VMEM(v, BF16) for v in (tail, tail, dense_tail, dense_tail, dense_tail, dense_tail, tail, tail)),
             pltpu.VMEM(mode_shapes.shape, BF16), pltpu.VMEM((64, modes), F32),
             pltpu.VMEM((ns,) + piece, F32), pltpu.VMEM((ns,) + piece, F32),
             pltpu.VMEM(piece, F32), pltpu.VMEM((ny,) + piece, F32),
             pltpu.VMEM(piece, F32), pltpu.VMEM((nz,) + piece, F32), pltpu.VMEM((ns,) + piece, F32),
-            pltpu.VMEM(dense, BF16), pltpu.VMEM(dense, BF16), pltpu.VMEM((elems, 256), BF16),
-            pltpu.VMEM(pair, BF16), pltpu.VMEM(pair, BF16), pltpu.VMEM((256, rows), F32),
-            dma((n,)), dma((n,)), dma((n,)), dma((n,)), dma((n,)), dma((n,)),
+            pltpu.VMEM((elems, 256), BF16), pltpu.VMEM((n, 128, elems), BF16), pltpu.VMEM((128, rows), BF16),
+            *(dma((n,)) for _ in range(18)),
             dma((ns,)), dma((ns,)), dma((ny,)), dma((ny,)), dma((nz,)), dma((nz,)), dma((ns,)), dma((ns,)),
-            dma((n,)), dma((n,)), dma((n,)), dma((n,)), dma(()),
+            dma(()),
         ],
         compiler_params=pltpu.CompilerParams(
             collective_id=0, has_side_effects=True, vmem_limit_bytes=56 * 1024 * 1024),

time: 152 us -> 145 us (0.954)
  Pallas kernels: 148 us -> 140 us
    pallas_call x1, Pallas kernels: 148 us -> 140 us  [fast(): pl.pallas_call(functools.partial(fused_kernel, n, ny, ns, scale), out_sha...]
where the time goes in v3:
time: 145 us; the launch traced here: 144 us
  Pallas kernels  140 us (97%)
  local copies, waits for them, and re-layouts  2.06 us (1%)
  between operations  1.99 us (1%)
    pallas_call x1, Pallas kernels, fast(): pl.pallas_call(functools.partial(fused_kernel, n, ny, ns, scale), out_sha...  140 us

profile of v3, /device:TPU:32, one launch (start us, length us, event | category | flops | bytes accessed | tf_op | source)
XLA Modules:
  0.0 144.1 jit_solution(11237315724458814253)
XLA Ops:
  0.6 0.0 copy-start.1
  0.6 0.0 copy-start.2
  0.6 0.0 copy-start.4
  0.7 139.8 %shard_map.81 = (bf16[192,2048]{1,0:T(8,128)(2,1)S(1)}, f32[64,512]{1,0:T(8,128)S(1)}) custom-call(s32[1,2048]{1,0:T(1,128)} %bitcast.76, s32[1,2048]{1,0:T(1,128)} %bitcast.84, f32[1,2048]{1,0:T(1,128)} %bitcast.82, bf16[192,2048]{1,0:T(8,128)(2,1)} %bitcast.68, f32[1,512]{1,0:T(1,128)} %bitcast.83, bf16[3,2048,512]{2,1,0:T(8,128)(2,1)} %mode_ref.1), custom_call_target="tpu_custom_call" | custom-call | flops 30000001024 | bytes 10000000 | tf_op jit(solution)/shard_map/pallas_call | solution.py:540
  140.5 0.5 slice.16
  142.3 0.0 copy-done.1
  142.3 0.0 copy-done.2
  142.3 0.0 copy-done.4
  142.3 0.2 conditional.1
  142.5 0.9 copy.93
  143.4 0.7 copy.94
Async XLA Ops:
  0.6 141.6 %copy-start.1 = (bf16[2048,192]{0,1:T(8,128)(2,1)S(1)}, bf16[2048,192]{0,1:T(8,128)(2,1)}, u32[]{:S(2)}) copy-start(bf16[2048,192]{0,1:T(8,128)(2,1)} %param.10) | copy-start | bytes 2359300
  0.6 141.6 %copy-start.2 = (s32[2048,1]{0,1:T(1,128)S(1)}, s32[2048,1]{0,1:T(1,128)}, u32[]{:S(2)}) copy-start(s32[2048,1]{0,1:T(1,128)} %param.11) | copy-start | bytes 24580
  0.6 141.6 %copy-start.4 = (f32[512]{0:T(512)S(1)}, f32[512]{0:T(512)}, u32[]{:S(2)}) copy-start(f32[512]{0:T(512)} %param.15) | copy-start | bytes 6148

commit v4 on v3

--- a/solution.py
+++ b/solution.py
@@ -173,15 +173,18 @@
     elem = elem_ref[...]
     cls = ((elem >> 6) + owner) & (n - 1)
     upper = (iota((256, 256), 0) < iota((256, 256), 1)).astype(BF16)
+    parts = [slice(256 * q, 256 * q + 256) for q in range(count // 256)]
+    hits = [one_hot(cls[:, part], n) for part in parts]
+    hits = jnp.concatenate(hits, axis=0)
+    before = mm(hits, upper)
+    hits = hits.astype(F32)
+    sums = jnp.sum(hits, axis=1, keepdims=True)
     base = jnp.zeros((n, 1), F32)
-    for q in range(count // 256):
-        part = cls[:, 256 * q : 256 * q + 256]
-        hit = iota((n, 256), 0) == jnp.broadcast_to(part, (n, 256))
-        hit_f = hit.astype(F32)
-        before = mm(hit_f.astype(BF16), upper) + base
-        rank = jnp.sum(jnp.where(hit, before, 0.0), axis=0, keepdims=True).astype(I32)
-        slot_ref[:, 256 * q : 256 * q + 256] = jnp.where(rank < CLASS_CAP, part * 128 + rank, -1)
-        base = base + jnp.sum(hit_f, axis=1, keepdims=True)
+    for q, part in enumerate(parts):
+        own = slice(n * q, n * q + n)
+        rank = jnp.sum(hits[own] * (before[own] + base), axis=0, keepdims=True).astype(I32)
+        slot_ref[:, part] = jnp.where(rank < CLASS_CAP, cls[:, part] * 128 + rank, -1)
+        base = base + sums[own]
     most = jnp.max(base, axis=0, keepdims=True)
     poison_ref[...] = jnp.broadcast_to(jnp.where(most > CLASS_CAP, jnp.nan, 0.0), (8, 128))
 
@@ -443,36 +446,36 @@
         return 0
 
     def gather(g, _):
-        sources = [cfd_peer(g * 4 + u) for u in range(4)]
+        sources = [cfd_peer(g * 8 + u) for u in range(8)]
         y4 = mm(jnp.concatenate([picks[src] for src in sources], axis=0), disp[:, 0:128])
         for u, src in enumerate(sources):
             send4[src] = y4[128 * u : 128 * u + CLASS_CAP].astype(BF16)
 
-            @pl.when(g * 4 + u > 0)
+            @pl.when(g * 8 + u > 0)
             def _():
                 hop4(src, me).start()
 
         return 0
 
     def gather_tail(g, _):
-        sources = [cfd_peer(g * 4 + u) for u in range(4)]
+        sources = [cfd_peer(g * 8 + u) for u in range(8)]
         y4 = mm(jnp.concatenate([picks[src] for src in sources], axis=0), disp[:, 128:256])
         keep = iota((64, 128), 1) < 64
         for u, src in enumerate(sources):
             y = y4[128 * u : 128 * u + 128]
             send4t[src] = jnp.where(keep, y[0:64], y[64:128]).astype(BF16)
 
-            @pl.when(g * 4 + u > 0)
+            @pl.when(g * 8 + u > 0)
             def _():
                 hop4t(src, me).start()
 
         return 0
 
     lax.fori_loop(0, n, unpack3, 0)
-    lax.fori_loop(0, n // 4, gather, 0)
+    lax.fori_loop(0, n // 8, gather, 0)
     recv4[me] = send4[me]
     lax.fori_loop(0, n, unpack3_tail, 0)
-    lax.fori_loop(0, n // 4, gather_tail, 0)
+    lax.fori_loop(0, n // 8, gather_tail, 0)
     recv4t[me] = send4t[me]
 
     acc_t[...] = jnp.zeros_like(acc_t)

time: 145 us -> 145 us (level)
  no operation moved by 1% of the time
where the time goes in v4:
time: 145 us; the launch traced here: 144 us
  Pallas kernels  139 us (96%)
  local copies, waits for them, and re-layouts  2.06 us (1%)
  between operations  1.99 us (1%)
    pallas_call x1, Pallas kernels, fast(): pl.pallas_call(functools.partial(fused_kernel, n, ny, ns, scale), out_sha...  139 us

profile of v4, /device:TPU:32, one launch (start us, length us, event | category | flops | bytes accessed | tf_op | source)
XLA Modules:
  0.0 143.7 jit_solution(15823260786959838999)
XLA Ops:
  0.6 0.0 copy-start.1
  0.6 0.0 copy-start.2
  0.6 0.0 copy-start.4
  0.7 139.4 %shard_map.81 = (bf16[192,2048]{1,0:T(8,128)(2,1)S(1)}, f32[64,512]{1,0:T(8,128)S(1)}) custom-call(s32[1,2048]{1,0:T(1,128)} %bitcast.76, s32[1,2048]{1,0:T(1,128)} %bitcast.84, f32[1,2048]{1,0:T(1,128)} %bitcast.82, bf16[192,2048]{1,0:T(8,128)(2,1)} %bitcast.68, f32[1,512]{1,0:T(1,128)} %bitcast.83, bf16[3,2048,512]{2,1,0:T(8,128)(2,1)} %mode_ref.1), custom_call_target="tpu_custom_call" | custom-call | flops 30000001024 | bytes 10000000 | tf_op jit(solution)/shard_map/pallas_call | solution.py:543
  140.1 0.5 slice.16
  141.9 0.0 copy-done.1
  141.9 0.0 copy-done.2
  141.9 0.0 copy-done.4
  142.0 0.2 conditional.1
  142.2 0.9 copy.93
  143.1 0.7 copy.94
Async XLA Ops:
  0.6 141.3 %copy-start.1 = (bf16[2048,192]{0,1:T(8,128)(2,1)S(1)}, bf16[2048,192]{0,1:T(8,128)(2,1)}, u32[]{:S(2)}) copy-start(bf16[2048,192]{0,1:T(8,128)(2,1)} %param.10) | copy-start | bytes 2359300
  0.6 141.3 %copy-start.2 = (s32[2048,1]{0,1:T(1,128)S(1)}, s32[2048,1]{0,1:T(1,128)}, u32[]{:S(2)}) copy-start(s32[2048,1]{0,1:T(1,128)} %param.11) | copy-start | bytes 24580
  0.6 141.3 %copy-start.4 = (f32[512]{0:T(512)S(1)}, f32[512]{0:T(512)}, u32[]{:S(2)}) copy-start(f32[512]{0:T(512)} %param.15) | copy-start | bytes 6148
